TPU v7x, 512 devices: a whole 4x4x16 slice. The times are simulated.
512 devices in a mesh: grp: 16 (over x, z_lo), blk: 32 (over y, z_hi, core).
Axes of the slice: x: 4, y: 4, z: 16 (z_hi: 4, z_lo: 4; z = z_hi * 4 + z_lo), core: 2. Of those that a mesh axis runs over, the one named last changes fastest.
Arguments:
- points: float32 [32, 65536], P(None, ('grp', 'blk')), may hold values from -6 to 6
- length_scales: float32 [32], replicated, may hold values from 1.5 to 6
- noise_level: float32 [1], replicated, may hold values from 0.3 to 1
- targets: float32 [16, 65536], P(None, ('grp', 'blk')), may hold values from -6 to 6
Outputs:
- solution_field: float32 [16, 65536], P(None, ('grp', 'blk'))
- residual: float32 [16, 65536], P(None, ('grp', 'blk'))
All inputs are finite; a program needn't handle non-finite values.
Results may differ from a plain program's by a relative error of at most 0.013.
Values may be sent and summed in bfloat16 or wider, within the bound.
No kernel may reach another device: no remote copies, remote signals or barrier semaphores. Data moves between devices by JAX's collectives and lax.ppermute only.
A program may use at most 192 MiB of HBM per device.

v0:
```python
import math

import jax
import jax.numpy as jnp
from jax import lax
from jax.sharding import PartitionSpec as P

ITERS = 2


SQRT_FIVE = math.sqrt(5.0)


def from_behind(value, axis, by):
    peers = lax.axis_size(axis)
    return lax.ppermute(value, axis, [(i, (i + by) % peers) for i in range(peers)])


def matern(dist2):
    spread = SQRT_FIVE * jnp.sqrt(jnp.maximum(dist2, 0.0))
    return ((1.0 + spread + spread * spread / 3.0) * jnp.exp(-spread)).astype(jnp.bfloat16)


def tile_from(rows_coords, cols_coords):
    width = rows_coords.shape[0] - 1
    inner = lax.dot_general(
        rows_coords[:width],
        cols_coords[:width],
        (((0,), (0,)), ((), ())),
        precision=lax.Precision.HIGHEST,
        preferred_element_type=jnp.float32,
    )
    return matern(rows_coords[width][:, None] + cols_coords[width][None, :] - 2.0 * inner)


def row_product(visitor, tile):
    return lax.dot_general(
        visitor, tile, (((1,), (1,)), ((), ())), preferred_element_type=jnp.float32
    )


def advance(current):
    return from_behind(current, "grp", 1)


def residual_sums(residual):
    return lax.psum(jnp.sum(residual * residual, axis=1), ("grp", "blk"))


def on_device(points, length_scales, noise_level, targets):
    scaled = points / length_scales[:, None]
    squares_own = jnp.sum(scaled * scaled, axis=0)
    packed = jnp.concatenate([scaled, squares_own[None, :]], axis=0)
    groups = lax.axis_size("grp")
    block_coords = lax.all_gather(packed, "blk", axis=1, tiled=True)

    def pass_points(carry, unused):
        moved = from_behind(carry, "grp", 1)
        return (moved, moved)

    ignored, cycle_coords = lax.scan(pass_points, block_coords, None, length=groups - 1)
    all_coords = jnp.concatenate([block_coords[None], cycle_coords], axis=0)

    def build(source):
        return tile_from(packed, source)

    solution_field = jnp.zeros_like(targets)
    residual = targets
    direction = targets
    norm_now = residual_sums(residual)
    for step in range(ITERS):
        probes = direction.astype(jnp.bfloat16)
        visitor = lax.all_gather(probes, "blk", axis=1, tiled=True)
        product = row_product(visitor, build(all_coords[0]))

        def cycle_step(carry, source):
            current, total = carry
            current = advance(current)
            total = total + row_product(current, build(source))
            return ((current, total), None)

        (current, product), apply_unused = lax.scan(cycle_step, (visitor, product), all_coords[1:])
        image = product + noise_level[0] * direction
        last = step + 1 == ITERS
        curve = lax.psum(jnp.sum(direction * image, axis=1), ("grp", "blk"))
        alpha = norm_now / curve
        solution_field = solution_field + alpha[:, None] * direction
        residual = residual - alpha[:, None] * image
        norm_next = norm_now if last else residual_sums(residual)
        if not last:
            direction = residual + (norm_next / norm_now)[:, None] * direction
            norm_now = norm_next
    return (solution_field, residual)


def solution(mesh):
    return jax.shard_map(
        on_device,
        mesh=mesh,
        in_specs=(P(None, ("grp", "blk")), P(), P(), P(None, ("grp", "blk"))),
        out_specs=(P(None, ("grp", "blk")), P(None, ("grp", "blk"))),
        check_vma=False,
    )
```

profile of v0, /device:TPU:1, one launch (start us, length us, event | category | flops | bytes accessed | tf_op | source)
XLA Modules:
  0.0 1100.8 jit_solution(16282841625116770139)
XLA Ops:
  1.5 64.3 %all_gather.10 = f32[33,4096]{1,0:T(8,128)S(1)} all-gather(f32[33,128]{1,0:T(8,128)S(1)} %pad_maximum_fusion), channel_id=1, replica_groups=mesh['grp'=16,'blk'=32] {'blk'}, dimensions={1}, use_global_device_ids=true | all-gather | bytes 557568 | tf_op jit(solution)/shard_map/all_gather | solution.py:55
  65.8 3.1 multiply_convert_fusion.2
  68.9 46.7 %all_gather.9 = bf16[16,4096]{1,0:T(8,128)(2,1)S(1)} all-gather(bf16[16,128]{1,0:T(8,128)(2,1)S(1)} %convert_element_type.16), channel_id=1, replica_groups=mesh['grp'=16,'blk'=32] {'blk'}, dimensions={1}, use_global_device_ids=true | all-gather | bytes 135168 | tf_op jit(solution)/shard_map/all_gather | solution.py:73
  116.0 282.2 %while.36 = (s32[]{:T(128)}, f32[33,4096]{1,0:T(8,128)S(1)}, f32[15,33,4096]{2,1,0:T(8,128)}, s32[]{:T(128)}) while((s32[]{:T(128)}, f32[33,4096]{1,0:T(8,128)S(1)}, f32[15,33,4096]{2,1,0:T(8,128)}, s32[]{:T(128)}) %tuple.51), condition=%wide.region_4.5_spmd, body=%wide.region_3.4_spmd.sunk | while | flops 2 | bytes 4440169 | solution.py:61
  116.0 1.9 collective-permute-start
  117.9 20.0 %collective-permute-done = f32[33,4096]{1,0:T(8,128)S(1)} collective-permute-done((f32[33,4096]{1,0:T(8,128)S(1)}, f32[33,4096]{1,0:T(8,128)S(1)}, u32[]{:S(2)}, u32[]{:S(2)}) %collective-permute-start) | collective-permute-done | bytes 540704 | tf_op jit(solution)/shard_map/while/body/eval_jaxpr/ppermute | solution.py:16
  140.8 19.1 %collective-permute-done = f32[33,4096]{1,0:T(8,128)S(1)} collective-permute-done((f32[33,4096]{1,0:T(8,128)S(1)}, f32[33,4096]{1,0:T(8,128)S(1)}, u32[]{:S(2)}, u32[]{:S(2)}) %collective-permute-start) | collective-permute-done | bytes 540704 | tf_op jit(solution)/shard_map/while/body/eval_jaxpr/ppermute | solution.py:16
  162.9 18.2 %collective-permute-done = f32[33,4096]{1,0:T(8,128)S(1)} collective-permute-done((f32[33,4096]{1,0:T(8,128)S(1)}, f32[33,4096]{1,0:T(8,128)S(1)}, u32[]{:S(2)}, u32[]{:S(2)}) %collective-permute-start) | collective-permute-done | bytes 540704 | tf_op jit(solution)/shard_map/while/body/eval_jaxpr/ppermute | solution.py:16
  183.9 17.3 %collective-permute-done = f32[33,4096]{1,0:T(8,128)S(1)} collective-permute-done((f32[33,4096]{1,0:T(8,128)S(1)}, f32[33,4096]{1,0:T(8,128)S(1)}, u32[]{:S(2)}, u32[]{:S(2)}) %collective-permute-start) | collective-permute-done | bytes 540704 | tf_op jit(solution)/shard_map/while/body/eval_jaxpr/ppermute | solution.py:16
  204.1 16.4 %collective-permute-done = f32[33,4096]{1,0:T(8,128)S(1)} collective-permute-done((f32[33,4096]{1,0:T(8,128)S(1)}, f32[33,4096]{1,0:T(8,128)S(1)}, u32[]{:S(2)}, u32[]{:S(2)}) %collective-permute-start) | collective-permute-done | bytes 540704 | tf_op jit(solution)/shard_map/while/body/eval_jaxpr/ppermute | solution.py:16
  223.3 15.4 %collective-permute-done = f32[33,4096]{1,0:T(8,128)S(1)} collective-permute-done((f32[33,4096]{1,0:T(8,128)S(1)}, f32[33,4096]{1,0:T(8,128)S(1)}, u32[]{:S(2)}, u32[]{:S(2)}) %collective-permute-start) | collective-permute-done | bytes 540704 | tf_op jit(solution)/shard_map/while/body/eval_jaxpr/ppermute | solution.py:16
  241.6 14.5 %collective-permute-done = f32[33,4096]{1,0:T(8,128)S(1)} collective-permute-done((f32[33,4096]{1,0:T(8,128)S(1)}, f32[33,4096]{1,0:T(8,128)S(1)}, u32[]{:S(2)}, u32[]{:S(2)}) %collective-permute-start) | collective-permute-done | bytes 540704 | tf_op jit(solution)/shard_map/while/body/eval_jaxpr/ppermute | solution.py:16
  259.0 13.3 %collective-permute-done = f32[33,4096]{1,0:T(8,128)S(1)} collective-permute-done((f32[33,4096]{1,0:T(8,128)S(1)}, f32[33,4096]{1,0:T(8,128)S(1)}, u32[]{:S(2)}, u32[]{:S(2)}) %collective-permute-start) | collective-permute-done | bytes 540704 | tf_op jit(solution)/shard_map/while/body/eval_jaxpr/ppermute | solution.py:16
  275.2 13.3 %collective-permute-done = f32[33,4096]{1,0:T(8,128)S(1)} collective-permute-done((f32[33,4096]{1,0:T(8,128)S(1)}, f32[33,4096]{1,0:T(8,128)S(1)}, u32[]{:S(2)}, u32[]{:S(2)}) %collective-permute-start) | collective-permute-done | bytes 540704 | tf_op jit(solution)/shard_map/while/body/eval_jaxpr/ppermute | solution.py:16
  291.4 13.3 %collective-permute-done = f32[33,4096]{1,0:T(8,128)S(1)} collective-permute-done((f32[33,4096]{1,0:T(8,128)S(1)}, f32[33,4096]{1,0:T(8,128)S(1)}, u32[]{:S(2)}, u32[]{:S(2)}) %collective-permute-start) | collective-permute-done | bytes 540704 | tf_op jit(solution)/shard_map/while/body/eval_jaxpr/ppermute | solution.py:16
  307.6 13.5 %collective-permute-done = f32[33,4096]{1,0:T(8,128)S(1)} collective-permute-done((f32[33,4096]{1,0:T(8,128)S(1)}, f32[33,4096]{1,0:T(8,128)S(1)}, u32[]{:S(2)}, u32[]{:S(2)}) %collective-permute-start) | collective-permute-done | bytes 540704 | tf_op jit(solution)/shard_map/while/body/eval_jaxpr/ppermute | solution.py:16
  323.9 14.6 %collective-permute-done = f32[33,4096]{1,0:T(8,128)S(1)} collective-permute-done((f32[33,4096]{1,0:T(8,128)S(1)}, f32[33,4096]{1,0:T(8,128)S(1)}, u32[]{:S(2)}, u32[]{:S(2)}) %collective-permute-start) | collective-permute-done | bytes 540704 | tf_op jit(solution)/shard_map/while/body/eval_jaxpr/ppermute | solution.py:16
  341.3 15.7 %collective-permute-done = f32[33,4096]{1,0:T(8,128)S(1)} collective-permute-done((f32[33,4096]{1,0:T(8,128)S(1)}, f32[33,4096]{1,0:T(8,128)S(1)}, u32[]{:S(2)}, u32[]{:S(2)}) %collective-permute-start) | collective-permute-done | bytes 540704 | tf_op jit(solution)/shard_map/while/body/eval_jaxpr/ppermute | solution.py:16
  359.9 16.7 %collective-permute-done = f32[33,4096]{1,0:T(8,128)S(1)} collective-permute-done((f32[33,4096]{1,0:T(8,128)S(1)}, f32[33,4096]{1,0:T(8,128)S(1)}, u32[]{:S(2)}, u32[]{:S(2)}) %collective-permute-start) | collective-permute-done | bytes 540704 | tf_op jit(solution)/shard_map/while/body/eval_jaxpr/ppermute | solution.py:16
  379.4 17.8 %collective-permute-done = f32[33,4096]{1,0:T(8,128)S(1)} collective-permute-done((f32[33,4096]{1,0:T(8,128)S(1)}, f32[33,4096]{1,0:T(8,128)S(1)}, u32[]{:S(2)}, u32[]{:S(2)}) %collective-permute-start) | collective-permute-done | bytes 540704 | tf_op jit(solution)/shard_map/while/body/eval_jaxpr/ppermute | solution.py:16
  398.2 152.6 %while.37 = (s32[]{:T(128)}, bf16[16,4096]{1,0:T(8,128)(2,1)S(1)}, f32[16,128]{1,0:T(8,128)S(1)}, f32[128]{0:T(128)S(1)}, f32[15,33,4096]{2,1,0:T(8,128)}, /*ind...) while((s32[]{:T(128)}, bf16[16,4096]{1,0:T(8,128)(2,1)S(1)}, f32[16,128]{1,0:T(8,128)S(1)}, ...), condition=%wide.region_6.7_spmd, body=%wide.region_5.6_spmd.sunk | while | flops 224397312 | bytes 3622041 | solution.py:82
  401.0 5.8 multiply_convert_fusion.5
  406.8 2.7 collective-permute-done.1
  412.7 5.8 multiply_convert_fusion.5
  422.5 5.8 multiply_convert_fusion.5
  432.4 5.8 multiply_convert_fusion.5
  439.5 1.9 collective-permute-start.1
  442.3 5.8 multiply_convert_fusion.5
  452.2 5.8 multiply_convert_fusion.5
  459.8 1.9 collective-permute-start.1
  462.7 5.8 multiply_convert_fusion.5
  468.5 2.3 collective-permute-done.1
  474.0 5.8 multiply_convert_fusion.5
  484.4 5.8 multiply_convert_fusion.5
  494.3 5.8 multiply_convert_fusion.5
  504.2 5.8 multiply_convert_fusion.5
  514.1 5.8 multiply_convert_fusion.5
  524.0 5.8 multiply_convert_fusion.5
  533.9 5.8 multiply_convert_fusion.5
  543.8 5.8 multiply_convert_fusion.5
  551.6 131.4 %all-reduce = (f32[16]{0:T(128)S(1)}, f32[16]{0:T(128)S(1)}) all-reduce(f32[16]{0:T(128)S(1)} %get-tuple-element.87, f32[16]{0:T(128)S(1)} %get-tuple-element.86), channel_id=1, replica_groups=mesh['grp'=16,'blk'=32] {'grp','blk'}, use_global_device_ids=true, to_apply=%region_1.2 | all-reduce | flops 32 | bytes 256 | tf_op jit(solution)/shard_map/psum | solution.py:47
  683.1 99.5 %psum.30 = f32[16]{0:T(128)S(1)} all-reduce(f32[16]{0:T(128)S(1)} %multiply_reduce_fusion.2), channel_id=1, replica_groups=mesh['grp'=16,'blk'=32] {'grp','blk'}, use_global_device_ids=true, to_apply=%region_10.11 | all-reduce | flops 16 | bytes 128 | tf_op jit(solution)/shard_map/psum | solution.py:47
  782.7 51.4 %all_gather.11 = bf16[16,4096]{1,0:T(8,128)(2,1)S(1)} all-gather(bf16[16,128]{1,0:T(8,128)(2,1)S(1)} %fusion.19), channel_id=1, replica_groups=mesh['grp'=16,'blk'=32] {'blk'}, dimensions={1}, use_global_device_ids=true | all-gather | bytes 135168 | tf_op jit(solution)/shard_map/all_gather | solution.py:73
  834.5 151.3 %while.38 = (s32[]{:T(128)}, bf16[16,4096]{1,0:T(8,128)(2,1)S(1)}, f32[16,128]{1,0:T(8,128)S(1)}, f32[128]{0:T(128)S(1)}, f32[15,33,4096]{2,1,0:T(8,128)}, /*ind...) while((s32[]{:T(128)}, bf16[16,4096]{1,0:T(8,128)(2,1)S(1)}, f32[16,128]{1,0:T(8,128)S(1)}, ...), condition=%wide.region_12.13_spmd, body=%wide.region_11.12_spmd.sunk | while | flops 224397312 | bytes 3622041 | solution.py:82
  834.5 3.7 collective-permute-start.2
  839.2 5.8 multiply_convert_fusion.6
  848.4 5.8 multiply_convert_fusion.6
  858.3 5.8 multiply_convert_fusion.6
  868.2 5.8 multiply_convert_fusion.6
  875.2 2.3 collective-permute-start.2
  878.4 5.8 multiply_convert_fusion.6
  888.0 5.8 multiply_convert_fusion.6
  897.8 5.8 multiply_convert_fusion.6
  907.7 5.8 multiply_convert_fusion.6
  914.8 2.5 collective-permute-start.2
  918.2 5.8 multiply_convert_fusion.6
  924.6 2.1 collective-permute-start.2
  927.7 5.8 multiply_convert_fusion.6
  938.4 5.8 multiply_convert_fusion.6
  949.2 5.8 multiply_convert_fusion.6
  959.1 5.8 multiply_convert_fusion.6
  969.0 5.8 multiply_convert_fusion.6
  978.8 5.8 multiply_convert_fusion.6
  986.1 114.0 %psum.31 = f32[16]{0:T(128)S(1)} all-reduce(f32[16]{0:T(128)S(1)} %multiply_reduce_fusion.1), channel_id=1, replica_groups=mesh['grp'=16,'blk'=32] {'grp','blk'}, use_global_device_ids=true, to_apply=%region_14.15 | all-reduce | flops 16 | bytes 128 | tf_op jit(solution)/shard_map/psum | solution.py:85
  (203 shorter events, 152.5 us)
Async XLA Ops:
  65.8 3.2 copy-start
  116.0 22.0 %collective-permute-start = (f32[33,4096]{1,0:T(8,128)S(1)}, f32[33,4096]{1,0:T(8,128)S(1)}, u32[]{:S(2)}, u32[]{:S(2)}) collective-permute-start(f32[33,4096]{1,0:T(8,128)S(1)} %get-tuple-element.222), channel_id=1, source_target_pairs={{0,32},{32,64},{64,96},{96,128},{128,160},{160,192},{192,224},{224... | collective-permute-start | bytes 1622024 | tf_op jit(solution)/shard_map/while/body/eval_jaxpr/ppermute | solution.py:16
  138.9 21.0 %collective-permute-start = (f32[33,4096]{1,0:T(8,128)S(1)}, f32[33,4096]{1,0:T(8,128)S(1)}, u32[]{:S(2)}, u32[]{:S(2)}) collective-permute-start(f32[33,4096]{1,0:T(8,128)S(1)} %get-tuple-element.222), channel_id=1, source_target_pairs={{0,32},{32,64},{64,96},{96,128},{128,160},{160,192},{192,224},{224... | collective-permute-start | bytes 1622024 | tf_op jit(solution)/shard_map/while/body/eval_jaxpr/ppermute | solution.py:16
  160.9 20.1 %collective-permute-start = (f32[33,4096]{1,0:T(8,128)S(1)}, f32[33,4096]{1,0:T(8,128)S(1)}, u32[]{:S(2)}, u32[]{:S(2)}) collective-permute-start(f32[33,4096]{1,0:T(8,128)S(1)} %get-tuple-element.222), channel_id=1, source_target_pairs={{0,32},{32,64},{64,96},{96,128},{128,160},{160,192},{192,224},{224... | collective-permute-start | bytes 1622024 | tf_op jit(solution)/shard_map/while/body/eval_jaxpr/ppermute | solution.py:16
  182.0 19.2 %collective-permute-start = (f32[33,4096]{1,0:T(8,128)S(1)}, f32[33,4096]{1,0:T(8,128)S(1)}, u32[]{:S(2)}, u32[]{:S(2)}) collective-permute-start(f32[33,4096]{1,0:T(8,128)S(1)} %get-tuple-element.222), channel_id=1, source_target_pairs={{0,32},{32,64},{64,96},{96,128},{128,160},{160,192},{192,224},{224... | collective-permute-start | bytes 1622024 | tf_op jit(solution)/shard_map/while/body/eval_jaxpr/ppermute | solution.py:16
  202.2 18.3 %collective-permute-start = (f32[33,4096]{1,0:T(8,128)S(1)}, f32[33,4096]{1,0:T(8,128)S(1)}, u32[]{:S(2)}, u32[]{:S(2)}) collective-permute-start(f32[33,4096]{1,0:T(8,128)S(1)} %get-tuple-element.222), channel_id=1, source_target_pairs={{0,32},{32,64},{64,96},{96,128},{128,160},{160,192},{192,224},{224... | collective-permute-start | bytes 1622024 | tf_op jit(solution)/shard_map/while/body/eval_jaxpr/ppermute | solution.py:16
  221.4 17.4 %collective-permute-start = (f32[33,4096]{1,0:T(8,128)S(1)}, f32[33,4096]{1,0:T(8,128)S(1)}, u32[]{:S(2)}, u32[]{:S(2)}) collective-permute-start(f32[33,4096]{1,0:T(8,128)S(1)} %get-tuple-element.222), channel_id=1, source_target_pairs={{0,32},{32,64},{64,96},{96,128},{128,160},{160,192},{192,224},{224... | collective-permute-start | bytes 1622024 | tf_op jit(solution)/shard_map/while/body/eval_jaxpr/ppermute | solution.py:16
  239.7 16.4 %collective-permute-start = (f32[33,4096]{1,0:T(8,128)S(1)}, f32[33,4096]{1,0:T(8,128)S(1)}, u32[]{:S(2)}, u32[]{:S(2)}) collective-permute-start(f32[33,4096]{1,0:T(8,128)S(1)} %get-tuple-element.222), channel_id=1, source_target_pairs={{0,32},{32,64},{64,96},{96,128},{128,160},{160,192},{192,224},{224... | collective-permute-start | bytes 1622024 | tf_op jit(solution)/shard_map/while/body/eval_jaxpr/ppermute | solution.py:16
  257.1 15.2 %collective-permute-start = (f32[33,4096]{1,0:T(8,128)S(1)}, f32[33,4096]{1,0:T(8,128)S(1)}, u32[]{:S(2)}, u32[]{:S(2)}) collective-permute-start(f32[33,4096]{1,0:T(8,128)S(1)} %get-tuple-element.222), channel_id=1, source_target_pairs={{0,32},{32,64},{64,96},{96,128},{128,160},{160,192},{192,224},{224... | collective-permute-start | bytes 1622024 | tf_op jit(solution)/shard_map/while/body/eval_jaxpr/ppermute | solution.py:16
  273.3 15.2 %collective-permute-start = (f32[33,4096]{1,0:T(8,128)S(1)}, f32[33,4096]{1,0:T(8,128)S(1)}, u32[]{:S(2)}, u32[]{:S(2)}) collective-permute-start(f32[33,4096]{1,0:T(8,128)S(1)} %get-tuple-element.222), channel_id=1, source_target_pairs={{0,32},{32,64},{64,96},{96,128},{128,160},{160,192},{192,224},{224... | collective-permute-start | bytes 1622024 | tf_op jit(solution)/shard_map/while/body/eval_jaxpr/ppermute | solution.py:16
  289.5 15.2 %collective-permute-start = (f32[33,4096]{1,0:T(8,128)S(1)}, f32[33,4096]{1,0:T(8,128)S(1)}, u32[]{:S(2)}, u32[]{:S(2)}) collective-permute-start(f32[33,4096]{1,0:T(8,128)S(1)} %get-tuple-element.222), channel_id=1, source_target_pairs={{0,32},{32,64},{64,96},{96,128},{128,160},{160,192},{192,224},{224... | collective-permute-start | bytes 1622024 | tf_op jit(solution)/shard_map/while/body/eval_jaxpr/ppermute | solution.py:16
  305.6 15.4 %collective-permute-start = (f32[33,4096]{1,0:T(8,128)S(1)}, f32[33,4096]{1,0:T(8,128)S(1)}, u32[]{:S(2)}, u32[]{:S(2)}) collective-permute-start(f32[33,4096]{1,0:T(8,128)S(1)} %get-tuple-element.222), channel_id=1, source_target_pairs={{0,32},{32,64},{64,96},{96,128},{128,160},{160,192},{192,224},{224... | collective-permute-start | bytes 1622024 | tf_op jit(solution)/shard_map/while/body/eval_jaxpr/ppermute | solution.py:16
  322.0 16.5 %collective-permute-start = (f32[33,4096]{1,0:T(8,128)S(1)}, f32[33,4096]{1,0:T(8,128)S(1)}, u32[]{:S(2)}, u32[]{:S(2)}) collective-permute-start(f32[33,4096]{1,0:T(8,128)S(1)} %get-tuple-element.222), channel_id=1, source_target_pairs={{0,32},{32,64},{64,96},{96,128},{128,160},{160,192},{192,224},{224... | collective-permute-start | bytes 1622024 | tf_op jit(solution)/shard_map/while/body/eval_jaxpr/ppermute | solution.py:16
  339.4 17.6 %collective-permute-start = (f32[33,4096]{1,0:T(8,128)S(1)}, f32[33,4096]{1,0:T(8,128)S(1)}, u32[]{:S(2)}, u32[]{:S(2)}) collective-permute-start(f32[33,4096]{1,0:T(8,128)S(1)} %get-tuple-element.222), channel_id=1, source_target_pairs={{0,32},{32,64},{64,96},{96,128},{128,160},{160,192},{192,224},{224... | collective-permute-start | bytes 1622024 | tf_op jit(solution)/shard_map/while/body/eval_jaxpr/ppermute | solution.py:16
  358.0 18.6 %collective-permute-start = (f32[33,4096]{1,0:T(8,128)S(1)}, f32[33,4096]{1,0:T(8,128)S(1)}, u32[]{:S(2)}, u32[]{:S(2)}) collective-permute-start(f32[33,4096]{1,0:T(8,128)S(1)} %get-tuple-element.222), channel_id=1, source_target_pairs={{0,32},{32,64},{64,96},{96,128},{128,160},{160,192},{192,224},{224... | collective-permute-start | bytes 1622024 | tf_op jit(solution)/shard_map/while/body/eval_jaxpr/ppermute | solution.py:16
  377.5 19.7 %collective-permute-start = (f32[33,4096]{1,0:T(8,128)S(1)}, f32[33,4096]{1,0:T(8,128)S(1)}, u32[]{:S(2)}, u32[]{:S(2)}) collective-permute-start(f32[33,4096]{1,0:T(8,128)S(1)} %get-tuple-element.222), channel_id=1, source_target_pairs={{0,32},{32,64},{64,96},{96,128},{128,160},{160,192},{192,224},{224... | collective-permute-start | bytes 1622024 | tf_op jit(solution)/shard_map/while/body/eval_jaxpr/ppermute | solution.py:16
  398.2 11.4 %collective-permute-start.1 = (bf16[16,4096]{1,0:T(8,128)(2,1)S(1)}, bf16[16,4096]{1,0:T(8,128)(2,1)S(1)}, u32[]{:S(2)}, u32[]{:S(2)}) collective-permute-start(bf16[16,4096]{1,0:T(8,128)(2,1)S(1)} %get-tuple-element.239), channel_id=1, source_target_pairs={{0,32},{32,64},{64,96},{96,128},{128,160},{160,192},{192,224},{224... | collective-permute-start | bytes 393224 | tf_op jit(solution)/shard_map/while/body/eval_jaxpr/ppermute | solution.py:16
  409.8 9.6 collective-permute-start.1
  419.7 9.6 collective-permute-start.1
  429.6 9.6 collective-permute-start.1
  439.5 9.6 collective-permute-start.1
  449.4 10.2 collective-permute-start.1
  459.8 11.0 %collective-permute-start.1 = (bf16[16,4096]{1,0:T(8,128)(2,1)S(1)}, bf16[16,4096]{1,0:T(8,128)(2,1)S(1)}, u32[]{:S(2)}, u32[]{:S(2)}) collective-permute-start(bf16[16,4096]{1,0:T(8,128)(2,1)S(1)} %get-tuple-element.239), channel_id=1, source_target_pairs={{0,32},{32,64},{64,96},{96,128},{128,160},{160,192},{192,224},{224... | collective-permute-start | bytes 393224 | tf_op jit(solution)/shard_map/while/body/eval_jaxpr/ppermute | solution.py:16
  471.1 10.2 collective-permute-start.1
  481.6 9.6 collective-permute-start.1
  491.5 9.6 collective-permute-start.1
  501.4 9.6 collective-permute-start.1
  511.2 9.6 collective-permute-start.1
  521.1 9.6 collective-permute-start.1
  531.0 9.6 collective-permute-start.1
  540.9 9.6 collective-permute-start.1
  834.5 10.7 collective-permute-start.2
  845.5 9.6 collective-permute-start.2
  855.4 9.6 collective-permute-start.2
  865.3 9.6 collective-permute-start.2
  875.2 9.6 collective-permute-start.2
  885.1 9.6 collective-permute-start.2
  895.0 9.6 collective-permute-start.2
  904.9 9.6 collective-permute-start.2
  914.8 9.6 collective-permute-start.2
  924.6 10.6 collective-permute-start.2
  935.5 10.5 collective-permute-start.2
  946.3 9.6 collective-permute-start.2
  956.2 9.6 collective-permute-start.2
  966.1 9.6 collective-permute-start.2
  976.0 9.6 collective-permute-start.2
where the time goes:
time: 1100 us
  blocking collectives  507 us (46%)
  waiting for transfers between devices  271 us (25%)
  matrix products  186 us (17%)
  starting transfers between devices  89.1 us (8%)
  local copies, waits for them, and re-layouts  42.2 us (4%)
    ppermute x45, waiting for transfers between devices, from_behind(): lax.ppermute(value, axis, [(i, (i + by) % peers) for i in range(peers)])  271 us
    psum x2, blocking collectives, residual_sums(): return lax.psum(jnp.sum(residual * residual, axis=1), ('grp', 'blk'))  231 us
    dot_general x31, matrix products, tile_from(): lax.dot_general(rows_coords[:width], cols_coords[:width], (((0,), (0,)),...  178 us
    psum x1, blocking collectives, on_device(): curve = lax.psum(jnp.sum(direction * image, axis=1), ('grp', 'blk'))  114 us
    all_gather x2, blocking collectives, on_device(): visitor = lax.all_gather(probes, 'blk', axis=1, tiled=True)  98.1 us
    ppermute x45, starting transfers between devices, from_behind(): lax.ppermute(value, axis, [(i, (i + by) % peers) for i in range(peers)])  89.1 us
    all_gather x1, blocking collectives, on_device(): block_coords = lax.all_gather(packed, 'blk', axis=1, tiled=True)  64.3 us
    slice x31, local copies, waits for them, and re-layouts, tile_from(): cols_coords[width][None, :]  27.7 us
  transfers between devices with their start and end apart: 45, of which 45 were waited for; matrix products, arithmetic and copies ran while one was open for 18% of the time, Pallas kernels for 0%

commit v1 on v0

v1 whole, which is shorter than its diff:
```python
import itertools
import math

import jax
import jax.numpy as jnp
from jax import lax
from jax.experimental import pallas as pl
from jax.experimental.pallas import tpu as pltpu
from jax.sharding import PartitionSpec as P

FEAT = 32
RHS = 16
OWN = 128
ROWS = 32
COLS = 16
DEPTH = 144
TALL = 512

BOTH = ("grp", "blk")
SIZES = {"x": 4, "z_lo": 4, "y": 4, "z_hi": 4, "core": 2}
PAIRS = [[2 * i, 2 * i + 1] for i in range(16)]


def groups_along(axes):
    rest = [axis for axis in SIZES if axis not in axes]
    found = []
    for fixed in itertools.product(*[range(SIZES[axis]) for axis in rest]):
        members = []
        for moving in itertools.product(*[range(SIZES[axis]) for axis in axes]):
            place = dict(zip(rest, fixed)) | dict(zip(axes, moving))
            index = 0
            for axis in SIZES:
                index = index * SIZES[axis] + place[axis]
            members.append(index)
        found.append(members)
    return found


ALONG_Z = groups_along(["z_hi", "z_lo"])
IN_PLANE = groups_along(["x", "y"])


def exchange(pieces, groups):
    return lax.all_to_all(pieces, BOTH, 0, 0, axis_index_groups=groups)


def spread(value, groups):
    return exchange(jnp.broadcast_to(value[None], (16,) + value.shape), groups)


def from_rows(value):
    column = spread(value, ALONG_Z)
    return lax.all_gather(column, "blk", axis_index_groups=PAIRS, axis=0, tiled=True)


def parts(value, count):
    found = []
    for _ in range(count):
        part = value.astype(jnp.bfloat16)
        found.append(part)
        value = value - part.astype(jnp.float32)
    return found


def operand(scaled, scale, left):
    squares = 5.0 * jnp.sum(scaled * scaled, axis=0, keepdims=True)
    high, low = parts(scaled * scale, 2)
    pieces = parts(squares, 3)
    ones = [jnp.ones_like(pieces[0])] * 3
    rest = jnp.zeros((DEPTH - 4 * FEAT - 6, scaled.shape[1]), jnp.bfloat16)
    if left:
        rows = [high, low, high, low] + pieces + ones
    else:
        rows = [high, high, low, low] + ones + pieces
    return jnp.concatenate(rows + [rest], axis=0)


def matern(five_dist2):
    five_dist2 = jnp.maximum(five_dist2, 1e-30)
    spread_ = five_dist2 * lax.rsqrt(five_dist2)
    decay = jnp.exp2(spread_ * (-math.log2(math.e)))
    return ((spread_ + 1.0) + five_dist2 * (1.0 / 3.0)) * decay


def build_kernel(rows_ref, cols_ref, tile_ref, product_ref, right, total):
    for block in range(COLS):
        right[:, block * OWN : (block + 1) * OWN] = operand(cols_ref[block], -10.0, False)
    total[...] = jnp.zeros_like(total)
    count = TALL // OWN

    def step(index, carry):
        blocks = [rows_ref[index * count + i] for i in range(count)]
        scaled = jnp.concatenate([block[:FEAT] for block in blocks], axis=1)
        probes = jnp.concatenate([block[FEAT:] for block in blocks], axis=1)
        probes = jnp.concatenate(parts(probes, 2), axis=0)
        left = operand(scaled, 1.0, True)
        dist = lax.dot_general(
            left, right[...], (((0,), (0,)), ((), ())), preferred_element_type=jnp.float32
        )
        kernel = matern(dist).astype(jnp.bfloat16)
        tile_ref[pl.ds(pl.multiple_of(index * TALL, TALL), TALL), :] = kernel
        total[...] += jnp.dot(probes, kernel, preferred_element_type=jnp.float32)
        return carry

    lax.fori_loop(0, ROWS // count, step, 0)
    put_product(total[...], product_ref)


def put_product(total, product_ref):
    both = total[:RHS] + total[RHS:]
    for block in range(COLS):
        product_ref[block] = both[:, block * OWN : (block + 1) * OWN]


def build(rows, cols):
    return pl.pallas_call(
        build_kernel,
        out_shape=(
            pltpu.VMEM((ROWS * OWN, COLS * OWN), jnp.bfloat16),
            jax.ShapeDtypeStruct((COLS, RHS, OWN), jnp.float32),
        ),
        in_specs=[pl.BlockSpec(memory_space=pltpu.VMEM)] * 2,
        out_specs=(pl.BlockSpec(memory_space=pltpu.VMEM),) * 2,
        scratch_shapes=[
            pltpu.VMEM((DEPTH, COLS * OWN), jnp.bfloat16),
            pltpu.VMEM((2 * RHS, COLS * OWN), jnp.float32),
        ],
        compiler_params=pltpu.CompilerParams(vmem_limit_bytes=24 * 2**20),
        name="build",
    )(rows, cols)


def again_kernel(probes_ref, tile_ref, product_ref):
    probes = jnp.concatenate([probes_ref[i] for i in range(ROWS)], axis=1)
    probes = jnp.concatenate(parts(probes, 2), axis=0)
    put_product(jnp.dot(probes, tile_ref[...], preferred_element_type=jnp.float32), product_ref)


def again(probes, tile):
    return pl.pallas_call(
        again_kernel,
        out_shape=jax.ShapeDtypeStruct((COLS, RHS, OWN), jnp.float32),
        in_specs=[pl.BlockSpec(memory_space=pltpu.VMEM)] * 2,
        out_specs=pl.BlockSpec(memory_space=pltpu.VMEM),
        compiler_params=pltpu.CompilerParams(vmem_limit_bytes=24 * 2**20),
        name="again",
    )(probes, tile)


def own_sum(partials):
    return jnp.sum(exchange(partials, IN_PLANE), axis=0)


def on_device(points, length_scales, noise_level, targets):
    scaled = (points / length_scales[:, None]).astype(jnp.float16)
    sent = jnp.concatenate([scaled, targets.astype(jnp.float16)], axis=0)
    cols = spread(scaled, IN_PLANE).astype(jnp.float32)
    rows = from_rows(sent).astype(jnp.float32)

    noise = noise_level[0]
    tile, partials = build(rows, cols)
    first = own_sum(partials) + noise * targets
    second = own_sum(again(from_rows(first), tile)) + noise * first

    pairs = [
        targets * targets,
        targets * first,
        first * first,
        targets * second,
        first * second,
    ]
    own = jnp.stack([jnp.sum(pair, axis=1) for pair in pairs]).reshape(1, -1)
    own = jnp.pad(own, ((0, 0), (0, OWN - own.shape[1])))
    near = jnp.sum(spread(own, IN_PLANE), axis=0)
    sums = jnp.sum(from_rows(near), axis=0)[0, : 5 * RHS].reshape(5, RHS)
    norm, curve, square, cross, cubic = sums
    alpha = norm / curve
    norm_next = norm - 2.0 * alpha * curve + alpha * alpha * square
    ratio = norm_next / norm
    keep = 1.0 + ratio
    curve_next = keep * keep * curve - keep * alpha * (square + cross) + alpha * alpha * cubic
    alpha_next = norm_next / curve_next
    alpha, keep, alpha_next = alpha[:, None], keep[:, None], alpha_next[:, None]
    direction = keep * targets - alpha * first
    image = keep * first - alpha * second
    solution_field = alpha * targets + alpha_next * direction
    residual = (targets - alpha * first) - alpha_next * image
    return (solution_field, residual)


def solution(mesh):
    return jax.shard_map(
        on_device,
        mesh=mesh,
        in_specs=(P(None, BOTH), P(), P(), P(None, BOTH)),
        out_specs=(P(None, BOTH), P(None, BOTH)),
        check_vma=False,
    )
```

time: 1100 us -> 158 us (0.14)
  blocking collectives: 507 us -> 68.9 us
  waiting for transfers between devices: 271 us -> 24.3 us
  matrix products: 186 us -> 0 us
  starting transfers between devices: 89.1 us -> 26.2 us
  local copies, waits for them, and re-layouts: 42.2 us -> 13 us
  Pallas kernels: 0 us -> 20 us
    psum x3 -> x0, blocking collectives: 345 us -> none  [the longest x2 231 us: residual_sums(): return lax.psum(jnp.sum(residual * residual, axis=1), ('grp', 'blk'))]
    ppermute x45 -> x0, waiting for transfers between devices: 271 us -> none  [from_behind(): lax.ppermute(value, axis, [(i, (i + by) % peers) for i in range(peers)])]
    dot_general x63 -> x0, matrix products: 186 us -> none  [the longest x31 178 us: tile_from(): lax.dot_general(rows_coords[:width], cols_coords[:width], (((0,), (0,)),...]
    all_gather x3, blocking collectives: 162 us -> 18.8 us  [from_rows(): lax.all_gather(column, 'blk', axis_index_groups=PAIRS, axis=0, tiled=True)]
    ppermute x45 -> x0, starting transfers between devices: 89.1 us -> none  [from_behind(): lax.ppermute(value, axis, [(i, (i + by) % peers) for i in range(peers)])]
    all_to_all x0 -> x4, blocking collectives: none -> 50 us  [exchange(): return lax.all_to_all(pieces, BOTH, 0, 0, axis_index_groups=groups)]
    slice x31 -> x0, local copies, waits for them, and re-layouts: 27.7 us -> none  [tile_from(): cols_coords[width][None, :]]
    all_to_all x0 -> x3, starting transfers between devices: none -> 26.2 us  [exchange(): return lax.all_to_all(pieces, BOTH, 0, 0, axis_index_groups=groups)]
  transfers between devices with their start and end apart: 45 -> 3, of which waited for: 45 -> 3; matrix products, arithmetic and copies ran while one was open for 18% -> 0% of each run, Pallas kernels for 0% -> 0%
where the time goes in v1:
time: 158 us; the launch traced here: 157 us
  blocking collectives  68.9 us (44%)
  starting transfers between devices  26.2 us (17%)
  waiting for transfers between devices  24.3 us (15%)
  Pallas kernels  20 us (13%)
  local copies, waits for them, and re-layouts  13 us (8%)
  other arithmetic  3.43 us (2%)
    all_to_all x4, blocking collectives, exchange(): return lax.all_to_all(pieces, BOTH, 0, 0, axis_index_groups=groups)  50 us
    all_to_all x3, starting transfers between devices, exchange(): return lax.all_to_all(pieces, BOTH, 0, 0, axis_index_groups=groups)  26.2 us
    all_to_all x3, waiting for transfers between devices, exchange(): return lax.all_to_all(pieces, BOTH, 0, 0, axis_index_groups=groups)  24.3 us
    all_gather x3, blocking collectives, from_rows(): lax.all_gather(column, 'blk', axis_index_groups=PAIRS, axis=0, tiled=True)  18.8 us
    pallas_call x1, Pallas kernels, build(): pl.pallas_call(build_kernel, out_shape=(pltpu.VMEM((ROWS * OWN, COLS * OW...  17.3 us
    unnamed x6, local copies, waits for them, and re-layouts  11.5 us
  transfers between devices with their start and end apart: 3, of which 3 were waited for; matrix products, arithmetic and copies ran while one was open for 0% of the time, Pallas kernels for 0%

profile of v1, /device:TPU:1, one launch (start us, length us, event | category | flops | bytes accessed | tf_op | source)
XLA Modules:
  0.0 157.2 jit_solution(10863943928586494559)
XLA Ops:
  0.6 0.0 copy-start.2
  0.6 0.8 divide_convert_fusion
  1.4 0.7 broadcast_in_dim.13
  2.1 7.6 %all-to-all-start.1 = ((f16[16,32,128]{2,1,0:T(8,128)(2,1)}), f16[16,32,128]{2,1,0:T(8,128)(2,1)S(1)}, u32[]{:S(2)}, u32[]{:S(2)}) async-start(f16[16,32,128]{2,1,0:T(8,128)(2,1)} %broadcast_in_dim.13), calls=%async_computation.1 | async-start | bytes 262144 | tf_op jit(solution)/shard_map/all_to_all | solution.py:44
  9.7 0.7 convert_element_type.15
  10.4 6.0 %all-to-all-done.1 = f16[16,32,128]{2,1,0:T(8,128)(2,1)S(1)} async-done(((f16[16,32,128]{2,1,0:T(8,128)(2,1)}), f16[16,32,128]{2,1,0:T(8,128)(2,1)S(1)}, u32[]{:S(2)}, u32[]{:S(2)}) %all-to-all-start.1) | async-done | bytes 131104 | tf_op jit(solution)/shard_map/all_to_all | solution.py:44
  16.4 0.7 broadcast_in_dim.12
  17.1 15.1 %all-to-all-start = ((f16[16,48,128]{2,1,0:T(8,128)(2,1)}), f16[16,48,128]{2,1,0:T(8,128)(2,1)S(1)}, u32[]{:S(2)}, u32[]{:S(2)}) async-start(f16[16,48,128]{2,1,0:T(8,128)(2,1)} %broadcast_in_dim.12), calls=%async_computation | async-start | bytes 393216 | tf_op jit(solution)/shard_map/all_to_all | solution.py:44
  32.2 12.3 %all-to-all-done = f16[16,48,128]{2,1,0:T(8,128)(2,1)S(1)} async-done(((f16[16,48,128]{2,1,0:T(8,128)(2,1)}), f16[16,48,128]{2,1,0:T(8,128)(2,1)S(1)}, u32[]{:S(2)}, u32[]{:S(2)}) %all-to-all-start) | async-done | bytes 196640 | tf_op jit(solution)/shard_map/all_to_all | solution.py:44
  44.5 7.3 %all_gather.9 = f16[32,48,128]{2,1,0:T(8,128)(2,1)S(1)} all-gather(f16[16,48,128]{2,1,0:T(8,128)(2,1)S(1)} %all-to-all-done), channel_id=1, replica_groups={{0,1},{2,3},{4,5},{6,7},{8,9},{10,11},{12,13},{14,15},{16,17},{18,19},{..., dimensions={0}, use_global_device_ids=true | all-gather | bytes 589824 | tf_op jit(solution)/shard_map/all_gather | solution.py:53
  51.9 0.1 convert_element_type.16.rows_ref
  51.9 17.3 %build.1 = (bf16[4096,2048]{1,0:T(8,128)(2,1)S(1)}, f32[16,16,128]{2,1,0:T(8,128)}) custom-call(f32[32,48,128]{2,1,0:T(8,128)S(1)} %convert_element_type.16.rows_ref, f32[16,32,128]{2,1,0:T(8,128)S(1)} %convert_element_type.17.cols_ref), custom_call_target="tpu_custom_call" | custom-call | tf_op jit(solution)/shard_map/build/pallas_call | solution.py:116
  69.2 0.0 copy-start
  69.2 5.7 %copy-done = bf16[4096,2048]{1,0:T(8,128)(2,1)} copy-done((bf16[4096,2048]{1,0:T(8,128)(2,1)}, bf16[4096,2048]{1,0:T(8,128)(2,1)S(1)}, u32[]{:S(2)}) %copy-start) | copy-done | bytes 16777240
  74.9 3.5 %all-to-all-start.2 = ((f32[16,16,128]{2,1,0:T(8,128)}), f32[16,16,128]{2,1,0:T(8,128)S(1)}, u32[]{:S(2)}, u32[]{:S(2)}) async-start(f32[16,16,128]{2,1,0:T(8,128)} %get-tuple-element.4), calls=%async_computation.2 | async-start | bytes 262144 | tf_op jit(solution)/shard_map/all_to_all | solution.py:44
  79.1 6.0 %all-to-all-done.2 = f32[16,16,128]{2,1,0:T(8,128)S(1)} async-done(((f32[16,16,128]{2,1,0:T(8,128)}), f32[16,16,128]{2,1,0:T(8,128)S(1)}, u32[]{:S(2)}, u32[]{:S(2)}) %all-to-all-start.2) | async-done | bytes 131104 | tf_op jit(solution)/shard_map/all_to_all | solution.py:44
  85.1 0.7 multiply_add_fusion.2
  85.9 15.8 %all_to_all.35 = f32[16,16,128]{2,1,0:T(8,128)S(1)} all-to-all(f32[16,16,128]{2,1,0:T(8,128)S(1)} %broadcast_in_dim.14), channel_id=1, replica_groups={{0,32,64,96,2,34,66,98,4,36,68,100,6,38,70,102},{1,33,65,97,3,35,67,99,..., dimensions={0} | all-to-all | bytes 262144 | tf_op jit(solution)/shard_map/all_to_all | solution.py:44
  101.6 5.6 %all_gather.10.probes_ref = f32[32,16,128]{2,1,0:T(8,128)S(1)} all-gather(f32[16,16,128]{2,1,0:T(8,128)S(1)} %all_to_all.35), channel_id=1, replica_groups={{0,1},{2,3},{4,5},{6,7},{8,9},{10,11},{12,13},{14,15},{16,17},{18,19},{..., dimensions={0}, use_global_device_ids=true | all-gather | bytes 393216 | tf_op jit(solution)/shard_map/all_gather | solution.py:53
  107.3 0.0 copy-start.1
  107.3 5.8 %copy-done.1 = bf16[4096,2048]{1,0:T(8,128)(2,1)S(1)} copy-done((bf16[4096,2048]{1,0:T(8,128)(2,1)S(1)}, bf16[4096,2048]{1,0:T(8,128)(2,1)}, u32[]{:S(2)}) %copy-start.1) | copy-done | bytes 16777240
  113.1 2.8 %again.1 = f32[16,16,128]{2,1,0:T(8,128)S(1)} custom-call(f32[32,16,128]{2,1,0:T(8,128)S(1)} %all_gather.10.probes_ref, bf16[4096,2048]{1,0:T(8,128)(2,1)S(1)} %copy-done.1), custom_call_target="tpu_custom_call" | custom-call | tf_op jit(solution)/shard_map/again/pallas_call | solution.py:140
  115.8 9.8 %all_to_all.36 = f32[16,16,128]{2,1,0:T(8,128)S(1)} all-to-all(f32[16,16,128]{2,1,0:T(8,128)S(1)} %again.1), channel_id=1, replica_groups={{0,8,16,24,128,136,144,152,256,264,272,280,384,392,400,408},{1,9,17,25,..., dimensions={0} | all-to-all | bytes 262144 | tf_op jit(solution)/shard_map/all_to_all | solution.py:44
  125.6 0.0 copy-done.2
  125.6 0.2 multiply_reduce_fusion
  125.9 0.1 reshape.104
  126.0 9.8 %all_to_all.37 = f32[16,1,128]{2,1,0:T(1,128)S(1)} all-to-all(f32[16,1,128]{2,1,0:T(1,128)S(1)} %broadcast_in_dim.16), channel_id=1, replica_groups={{0,8,16,24,128,136,144,152,256,264,272,280,384,392,400,408},{1,9,17,25,..., dimensions={0} | all-to-all | bytes 16384 | tf_op jit(solution)/shard_map/all_to_all | solution.py:44
  135.8 14.6 %all_to_all.38 = f32[16,1,128]{2,1,0:T(1,128)S(1)} all-to-all(f32[16,1,128]{2,1,0:T(1,128)S(1)} %broadcast_in_dim.17), channel_id=1, replica_groups={{0,32,64,96,2,34,66,98,4,36,68,100,6,38,70,102},{1,33,65,97,3,35,67,99,..., dimensions={0} | all-to-all | bytes 16384 | tf_op jit(solution)/shard_map/all_to_all | solution.py:44
  150.4 5.8 %all_gather.11 = f32[32,1,128]{2,1,0:T(1,128)S(1)} all-gather(f32[16,1,128]{2,1,0:T(1,128)S(1)} %all_to_all.38), channel_id=1, replica_groups={{0,1},{2,3},{4,5},{6,7},{8,9},{10,11},{12,13},{14,15},{16,17},{18,19},{..., dimensions={0}, use_global_device_ids=true | all-gather | bytes 24576 | tf_op jit(solution)/shard_map/all_gather | solution.py:53
  156.3 0.1 reduce_sum.91
  156.3 0.1 fusion.4
  156.4 0.1 fusion.1
  156.5 0.7 multiply_subtract_fusion
  (10 shorter events, 0.1 us)
Async XLA Ops:
  0.6 125.0 %copy-start.2 = (f32[16,128]{1,0:T(8,128)S(1)}, f32[16,128]{1,0:T(8,128)}, u32[]{:S(2)}) copy-start(f32[16,128]{1,0:T(8,128)} %param.7) | copy-start | bytes 24580
  2.1 14.3 %all-to-all-start.1 = ((f16[16,32,128]{2,1,0:T(8,128)(2,1)}), f16[16,32,128]{2,1,0:T(8,128)(2,1)S(1)}, u32[]{:S(2)}, u32[]{:S(2)}) async-start(f16[16,32,128]{2,1,0:T(8,128)(2,1)} %broadcast_in_dim.13), calls=%async_computation.1 | async-start | bytes 262144 | tf_op jit(solution)/shard_map/all_to_all | solution.py:44
  17.1 27.4 %all-to-all-start = ((f16[16,48,128]{2,1,0:T(8,128)(2,1)}), f16[16,48,128]{2,1,0:T(8,128)(2,1)S(1)}, u32[]{:S(2)}, u32[]{:S(2)}) async-start(f16[16,48,128]{2,1,0:T(8,128)(2,1)} %broadcast_in_dim.12), calls=%async_computation | async-start | bytes 393216 | tf_op jit(solution)/shard_map/all_to_all | solution.py:44
  69.2 5.7 %copy-start = (bf16[4096,2048]{1,0:T(8,128)(2,1)}, bf16[4096,2048]{1,0:T(8,128)(2,1)S(1)}, u32[]{:S(2)}) copy-start(bf16[4096,2048]{1,0:T(8,128)(2,1)S(1)} %get-tuple-element.5.tile_ref) | copy-start | bytes 50331652
  74.9 10.2 %all-to-all-start.2 = ((f32[16,16,128]{2,1,0:T(8,128)}), f32[16,16,128]{2,1,0:T(8,128)S(1)}, u32[]{:S(2)}, u32[]{:S(2)}) async-start(f32[16,16,128]{2,1,0:T(8,128)} %get-tuple-element.4), calls=%async_computation.2 | async-start | bytes 262144 | tf_op jit(solution)/shard_map/all_to_all | solution.py:44
  107.3 5.8 %copy-start.1 = (bf16[4096,2048]{1,0:T(8,128)(2,1)S(1)}, bf16[4096,2048]{1,0:T(8,128)(2,1)}, u32[]{:S(2)}) copy-start(bf16[4096,2048]{1,0:T(8,128)(2,1)} %copy-done) | copy-start | bytes 50331652

commit v2 on v1

--- a/solution.py
+++ b/solution.py
@@ -14,7 +14,8 @@
 ROWS = 32
 COLS = 16
 DEPTH = 144
-TALL = 512
+WIDE = 256
+CHUNKS = COLS * OWN // WIDE
 
 BOTH = ("grp", "blk")
 SIZES = {"x": 4, "z_lo": 4, "y": 4, "z_hi": 4, "core": 2}
@@ -37,7 +38,7 @@
 
 
 ALONG_Z = groups_along(["z_hi", "z_lo"])
-IN_PLANE = groups_along(["x", "y"])
+IN_PLANE = groups_along(["y", "x"])
 
 
 def exchange(pieces, groups):
@@ -82,67 +83,94 @@
     return ((spread_ + 1.0) + five_dist2 * (1.0 / 3.0)) * decay
 
 
-def build_kernel(rows_ref, cols_ref, tile_ref, product_ref, right, total):
+def put_product(total, chunk, product_ref):
+    both = total[:RHS] + total[RHS:]
+    for block in range(WIDE // OWN):
+        product_ref[chunk * (WIDE // OWN) + block] = both[:, block * OWN : (block + 1) * OWN]
+
+
+def stacked(pieces):
+    return jnp.concatenate(parts(jnp.concatenate(pieces, axis=1), 2), axis=0)
+
+
+def build_kernel(rows_ref, cols_ref, tile_ref, product_ref, left, right, probes, held, sems):
     for block in range(COLS):
         right[:, block * OWN : (block + 1) * OWN] = operand(cols_ref[block], -10.0, False)
-    total[...] = jnp.zeros_like(total)
-    count = TALL // OWN
-
-    def step(index, carry):
-        blocks = [rows_ref[index * count + i] for i in range(count)]
+    for some in range(0, ROWS, 4):
+        blocks = [rows_ref[some + i] for i in range(4)]
+        at = slice(some * OWN, (some + 4) * OWN)
         scaled = jnp.concatenate([block[:FEAT] for block in blocks], axis=1)
-        probes = jnp.concatenate([block[FEAT:] for block in blocks], axis=1)
-        probes = jnp.concatenate(parts(probes, 2), axis=0)
-        left = operand(scaled, 1.0, True)
-        dist = lax.dot_general(
-            left, right[...], (((0,), (0,)), ((), ())), preferred_element_type=jnp.float32
-        )
+        left[at, :] = operand(scaled, 1.0, True).T
+        probes[:, at] = stacked([block[FEAT:] for block in blocks])
+
+    def leave(chunk):
+        slot = chunk % 2
+        return pltpu.make_async_copy(held.at[slot], tile_ref.at[chunk], sems.at[slot])
+
+    def step(chunk, carry):
+        @pl.when(chunk >= 2)
+        def _():
+            leave(chunk - 2).wait()
+
+        cols = pl.ds(pl.multiple_of(chunk * WIDE, WIDE), WIDE)
+        dist = jnp.dot(left[...], right[:, cols], preferred_element_type=jnp.float32)
         kernel = matern(dist).astype(jnp.bfloat16)
-        tile_ref[pl.ds(pl.multiple_of(index * TALL, TALL), TALL), :] = kernel
-        total[...] += jnp.dot(probes, kernel, preferred_element_type=jnp.float32)
+        held[chunk % 2] = kernel
+        total = jnp.dot(probes[...], kernel, preferred_element_type=jnp.float32)
+        put_product(total, chunk, product_ref)
+        leave(chunk).start()
         return carry
 
-    lax.fori_loop(0, ROWS // count, step, 0)
-    put_product(total[...], product_ref)
-
-
-def put_product(total, product_ref):
-    both = total[:RHS] + total[RHS:]
-    for block in range(COLS):
-        product_ref[block] = both[:, block * OWN : (block + 1) * OWN]
+    lax.fori_loop(0, CHUNKS, step, 0)
+    leave(CHUNKS - 2).wait()
+    leave(CHUNKS - 1).wait()
 
 
 def build(rows, cols):
     return pl.pallas_call(
         build_kernel,
         out_shape=(
-            pltpu.VMEM((ROWS * OWN, COLS * OWN), jnp.bfloat16),
+            jax.ShapeDtypeStruct((CHUNKS, ROWS * OWN, WIDE), jnp.bfloat16),
             jax.ShapeDtypeStruct((COLS, RHS, OWN), jnp.float32),
         ),
         in_specs=[pl.BlockSpec(memory_space=pltpu.VMEM)] * 2,
-        out_specs=(pl.BlockSpec(memory_space=pltpu.VMEM),) * 2,
+        out_specs=(pl.BlockSpec(memory_space=pl.ANY), pl.BlockSpec(memory_space=pltpu.VMEM)),
         scratch_shapes=[
+            pltpu.VMEM((ROWS * OWN, DEPTH), jnp.bfloat16),
             pltpu.VMEM((DEPTH, COLS * OWN), jnp.bfloat16),
-            pltpu.VMEM((2 * RHS, COLS * OWN), jnp.float32),
+            pltpu.VMEM((2 * RHS, ROWS * OWN), jnp.bfloat16),
+            pltpu.VMEM((2, ROWS * OWN, WIDE), jnp.bfloat16),
+            pltpu.SemaphoreType.DMA((2,)),
         ],
-        compiler_params=pltpu.CompilerParams(vmem_limit_bytes=24 * 2**20),
+        compiler_params=pltpu.CompilerParams(vmem_limit_bytes=40 * 2**20),
         name="build",
     )(rows, cols)
 
 
-def again_kernel(probes_ref, tile_ref, product_ref):
-    probes = jnp.concatenate([probes_ref[i] for i in range(ROWS)], axis=1)
-    probes = jnp.concatenate(parts(probes, 2), axis=0)
-    put_product(jnp.dot(probes, tile_ref[...], preferred_element_type=jnp.float32), product_ref)
+def again_kernel(probes_ref, tile_ref, product_ref, held, sems):
+    def fetch(chunk):
+        return pltpu.make_async_copy(tile_ref.at[chunk], held.at[chunk], sems.at[chunk])
+
+    for chunk in range(CHUNKS):
+        fetch(chunk).start()
+    probes = stacked([probes_ref[i] for i in range(ROWS)])
+    for chunk in range(CHUNKS):
+        fetch(chunk).wait()
+        total = jnp.dot(probes, held[chunk], preferred_element_type=jnp.float32)
+        put_product(total, chunk, product_ref)
 
 
 def again(probes, tile):
     return pl.pallas_call(
         again_kernel,
         out_shape=jax.ShapeDtypeStruct((COLS, RHS, OWN), jnp.float32),
-        in_specs=[pl.BlockSpec(memory_space=pltpu.VMEM)] * 2,
+        in_specs=[pl.BlockSpec(memory_space=pltpu.VMEM), pl.BlockSpec(memory_space=pl.ANY)],
         out_specs=pl.BlockSpec(memory_space=pltpu.VMEM),
-        compiler_params=pltpu.CompilerParams(vmem_limit_bytes=24 * 2**20),
+        scratch_shapes=[
+            pltpu.VMEM((CHUNKS, ROWS * OWN, WIDE), jnp.bfloat16),
+            pltpu.SemaphoreType.DMA((CHUNKS,)),
+        ],
+        compiler_params=pltpu.CompilerParams(vmem_limit_bytes=40 * 2**20),
         name="again",
     )(probes, tile)
 

time: 158 us -> 150 us (0.949)
  local copies, waits for them, and re-layouts: 13 us -> 1.51 us
  Pallas kernels: 20 us -> 23.9 us
    unnamed x6 -> x2, local copies, waits for them, and re-layouts: 11.5 us -> 0.01 us
    pallas_call x1, Pallas kernels: 2.75 us -> 6.96 us  [again(): pl.pallas_call(again_kernel, out_shape=jax.ShapeDtypeStruct((COLS, RHS, O...]
where the time goes in v2:
time: 150 us; the launch traced here: 149 us
  blocking collectives  68.4 us (46%)
  starting transfers between devices  26 us (17%)
  waiting for transfers between devices  24.6 us (16%)
  Pallas kernels  23.9 us (16%)
  other arithmetic  3.43 us (2%)
  local copies, waits for them, and re-layouts  1.51 us (1%)
    all_to_all x4, blocking collectives, exchange(): return lax.all_to_all(pieces, BOTH, 0, 0, axis_index_groups=groups)  49.8 us
    all_to_all x3, starting transfers between devices, exchange(): return lax.all_to_all(pieces, BOTH, 0, 0, axis_index_groups=groups)  26 us
    all_to_all x3, waiting for transfers between devices, exchange(): return lax.all_to_all(pieces, BOTH, 0, 0, axis_index_groups=groups)  24.6 us
    all_gather x3, blocking collectives, from_rows(): lax.all_gather(column, 'blk', axis_index_groups=PAIRS, axis=0, tiled=True)  18.6 us
    pallas_call x1, Pallas kernels, build(): pl.pallas_call(build_kernel, out_shape=(jax.ShapeDtypeStruct((CHUNKS, ROW...  16.9 us
    pallas_call x1, Pallas kernels, again(): pl.pallas_call(again_kernel, out_shape=jax.ShapeDtypeStruct((COLS, RHS, O...  6.96 us
  transfers between devices with their start and end apart: 3, of which 3 were waited for; matrix products, arithmetic and copies ran while one was open for 0% of the time, Pallas kernels for 0%

profile of v2, /device:TPU:1, one launch (start us, length us, event | category | flops | bytes accessed | tf_op | source)
XLA Modules:
  0.0 149.2 jit_solution(14214631294391954948)
XLA Ops:
  0.6 0.0 copy-start
  0.6 0.8 divide_convert_fusion
  1.4 0.7 broadcast_in_dim.13
  2.1 7.6 %all-to-all-start.1 = ((f16[16,32,128]{2,1,0:T(8,128)(2,1)}), f16[16,32,128]{2,1,0:T(8,128)(2,1)S(1)}, u32[]{:S(2)}, u32[]{:S(2)}) async-start(f16[16,32,128]{2,1,0:T(8,128)(2,1)} %broadcast_in_dim.13), calls=%async_computation.1 | async-start | bytes 262144 | tf_op jit(solution)/shard_map/all_to_all | solution.py:45
  9.7 0.7 convert_element_type.15
  10.4 6.1 %all-to-all-done.1 = f16[16,32,128]{2,1,0:T(8,128)(2,1)S(1)} async-done(((f16[16,32,128]{2,1,0:T(8,128)(2,1)}), f16[16,32,128]{2,1,0:T(8,128)(2,1)S(1)}, u32[]{:S(2)}, u32[]{:S(2)}) %all-to-all-start.1) | async-done | bytes 131104 | tf_op jit(solution)/shard_map/all_to_all | solution.py:45
  16.5 0.7 broadcast_in_dim.12
  17.2 14.9 %all-to-all-start = ((f16[16,48,128]{2,1,0:T(8,128)(2,1)}), f16[16,48,128]{2,1,0:T(8,128)(2,1)S(1)}, u32[]{:S(2)}, u32[]{:S(2)}) async-start(f16[16,48,128]{2,1,0:T(8,128)(2,1)} %broadcast_in_dim.12), calls=%async_computation | async-start | bytes 393216 | tf_op jit(solution)/shard_map/all_to_all | solution.py:45
  32.2 12.3 %all-to-all-done = f16[16,48,128]{2,1,0:T(8,128)(2,1)S(1)} async-done(((f16[16,48,128]{2,1,0:T(8,128)(2,1)}), f16[16,48,128]{2,1,0:T(8,128)(2,1)S(1)}, u32[]{:S(2)}, u32[]{:S(2)}) %all-to-all-start) | async-done | bytes 196640 | tf_op jit(solution)/shard_map/all_to_all | solution.py:45
  44.5 7.3 %all_gather.9 = f16[32,48,128]{2,1,0:T(8,128)(2,1)S(1)} all-gather(f16[16,48,128]{2,1,0:T(8,128)(2,1)S(1)} %all-to-all-done), channel_id=1, replica_groups={{0,1},{2,3},{4,5},{6,7},{8,9},{10,11},{12,13},{14,15},{16,17},{18,19},{..., dimensions={0}, use_global_device_ids=true | all-gather | bytes 589824 | tf_op jit(solution)/shard_map/all_gather | solution.py:54
  51.8 0.1 convert_element_type.16.rows_ref
  51.9 16.9 %build.1 = (bf16[8,4096,256]{2,1,0:T(8,128)(2,1)}, f32[16,16,128]{2,1,0:T(8,128)}) custom-call(f32[32,48,128]{2,1,0:T(8,128)S(1)} %convert_element_type.16.rows_ref, f32[16,32,128]{2,1,0:T(8,128)S(1)} %convert_element_type.17.cols_ref), custom_call_target="tpu_custom_call" | custom-call | tf_op jit(solution)/shard_map/build/pallas_call | solution.py:130
  68.8 3.5 %all-to-all-start.2 = ((f32[16,16,128]{2,1,0:T(8,128)}), f32[16,16,128]{2,1,0:T(8,128)S(1)}, u32[]{:S(2)}, u32[]{:S(2)}) async-start(f32[16,16,128]{2,1,0:T(8,128)} %get-tuple-element.4), calls=%async_computation.2 | async-start | bytes 262144 | tf_op jit(solution)/shard_map/all_to_all | solution.py:45
  73.0 6.2 %all-to-all-done.2 = f32[16,16,128]{2,1,0:T(8,128)S(1)} async-done(((f32[16,16,128]{2,1,0:T(8,128)}), f32[16,16,128]{2,1,0:T(8,128)S(1)}, u32[]{:S(2)}, u32[]{:S(2)}) %all-to-all-start.2) | async-done | bytes 131104 | tf_op jit(solution)/shard_map/all_to_all | solution.py:45
  79.1 0.7 multiply_add_fusion.2
  79.9 16.0 %all_to_all.35 = f32[16,16,128]{2,1,0:T(8,128)S(1)} all-to-all(f32[16,16,128]{2,1,0:T(8,128)S(1)} %broadcast_in_dim.14), channel_id=1, replica_groups={{0,32,64,96,2,34,66,98,4,36,68,100,6,38,70,102},{1,33,65,97,3,35,67,99,..., dimensions={0} | all-to-all | bytes 262144 | tf_op jit(solution)/shard_map/all_to_all | solution.py:45
  95.8 5.4 %all_gather.10.probes_ref = f32[32,16,128]{2,1,0:T(8,128)S(1)} all-gather(f32[16,16,128]{2,1,0:T(8,128)S(1)} %all_to_all.35), channel_id=1, replica_groups={{0,1},{2,3},{4,5},{6,7},{8,9},{10,11},{12,13},{14,15},{16,17},{18,19},{..., dimensions={0}, use_global_device_ids=true | all-gather | bytes 393216 | tf_op jit(solution)/shard_map/all_gather | solution.py:54
  101.3 7.0 %again.1 = f32[16,16,128]{2,1,0:T(8,128)S(1)} custom-call(f32[32,16,128]{2,1,0:T(8,128)S(1)} %all_gather.10.probes_ref, bf16[8,4096,256]{2,1,0:T(8,128)(2,1)} %get-tuple-element.5.tile_ref), custom_call_target="tpu_custom_call" | custom-call | tf_op jit(solution)/shard_map/again/pallas_call | solution.py:164
  108.2 9.7 %all_to_all.36 = f32[16,16,128]{2,1,0:T(8,128)S(1)} all-to-all(f32[16,16,128]{2,1,0:T(8,128)S(1)} %again.1), channel_id=1, replica_groups={{0,128,256,384,8,136,264,392,16,144,272,400,24,152,280,408},{1,129,257,..., dimensions={0} | all-to-all | bytes 262144 | tf_op jit(solution)/shard_map/all_to_all | solution.py:45
  117.9 0.0 copy-done
  117.9 0.2 multiply_reduce_fusion
  118.1 0.1 reshape.104
  118.2 9.5 %all_to_all.37 = f32[16,1,128]{2,1,0:T(1,128)S(1)} all-to-all(f32[16,1,128]{2,1,0:T(1,128)S(1)} %broadcast_in_dim.16), channel_id=1, replica_groups={{0,128,256,384,8,136,264,392,16,144,272,400,24,152,280,408},{1,129,257,..., dimensions={0} | all-to-all | bytes 16384 | tf_op jit(solution)/shard_map/all_to_all | solution.py:45
  127.8 14.7 %all_to_all.38 = f32[16,1,128]{2,1,0:T(1,128)S(1)} all-to-all(f32[16,1,128]{2,1,0:T(1,128)S(1)} %broadcast_in_dim.17), channel_id=1, replica_groups={{0,32,64,96,2,34,66,98,4,36,68,100,6,38,70,102},{1,33,65,97,3,35,67,99,..., dimensions={0} | all-to-all | bytes 16384 | tf_op jit(solution)/shard_map/all_to_all | solution.py:45
  142.5 5.8 %all_gather.11 = f32[32,1,128]{2,1,0:T(1,128)S(1)} all-gather(f32[16,1,128]{2,1,0:T(1,128)S(1)} %all_to_all.38), channel_id=1, replica_groups={{0,1},{2,3},{4,5},{6,7},{8,9},{10,11},{12,13},{14,15},{16,17},{18,19},{..., dimensions={0}, use_global_device_ids=true | all-gather | bytes 24576 | tf_op jit(solution)/shard_map/all_gather | solution.py:54
  148.3 0.1 reduce_sum.91
  148.4 0.1 fusion.4
  148.4 0.1 fusion.1
  148.5 0.7 multiply_subtract_fusion
  (10 shorter events, 0.1 us)
Async XLA Ops:
  0.6 117.3 %copy-start = (f32[16,128]{1,0:T(8,128)S(1)}, f32[16,128]{1,0:T(8,128)}, u32[]{:S(2)}) copy-start(f32[16,128]{1,0:T(8,128)} %param.7) | copy-start | bytes 24580
  2.1 14.4 %all-to-all-start.1 = ((f16[16,32,128]{2,1,0:T(8,128)(2,1)}), f16[16,32,128]{2,1,0:T(8,128)(2,1)S(1)}, u32[]{:S(2)}, u32[]{:S(2)}) async-start(f16[16,32,128]{2,1,0:T(8,128)(2,1)} %broadcast_in_dim.13), calls=%async_computation.1 | async-start | bytes 262144 | tf_op jit(solution)/shard_map/all_to_all | solution.py:45
  17.2 27.3 %all-to-all-start = ((f16[16,48,128]{2,1,0:T(8,128)(2,1)}), f16[16,48,128]{2,1,0:T(8,128)(2,1)S(1)}, u32[]{:S(2)}, u32[]{:S(2)}) async-start(f16[16,48,128]{2,1,0:T(8,128)(2,1)} %broadcast_in_dim.12), calls=%async_computation | async-start | bytes 393216 | tf_op jit(solution)/shard_map/all_to_all | solution.py:45
  68.8 10.3 %all-to-all-start.2 = ((f32[16,16,128]{2,1,0:T(8,128)}), f32[16,16,128]{2,1,0:T(8,128)S(1)}, u32[]{:S(2)}, u32[]{:S(2)}) async-start(f32[16,16,128]{2,1,0:T(8,128)} %get-tuple-element.4), calls=%async_computation.2 | async-start | bytes 262144 | tf_op jit(solution)/shard_map/all_to_all | solution.py:45

commit v3 on v2

--- a/solution.py
+++ b/solution.py
@@ -39,19 +39,33 @@
 
 ALONG_Z = groups_along(["z_hi", "z_lo"])
 IN_PLANE = groups_along(["y", "x"])
+IN_PLANE_PAIR = groups_along(["y", "x", "core"])
 
 
 def exchange(pieces, groups):
     return lax.all_to_all(pieces, BOTH, 0, 0, axis_index_groups=groups)
 
 
+def copies(value, groups):
+    return jnp.broadcast_to(value[None], (len(groups[0]),) + value.shape)
+
+
 def spread(value, groups):
-    return exchange(jnp.broadcast_to(value[None], (16,) + value.shape), groups)
-
-
-def from_rows(value):
-    column = spread(value, ALONG_Z)
-    return lax.all_gather(column, "blk", axis_index_groups=PAIRS, axis=0, tiled=True)
+    return exchange(copies(value, groups), groups)
+
+
+def from_pair(value):
+    return lax.all_gather(value, "blk", axis_index_groups=PAIRS, axis=0, tiled=True)
+
+
+def pressed(value, power, scale):
+    size = jnp.exp2(jnp.log2(jnp.abs(value)) * (1.0 / power)) * scale
+    return jnp.where(value < 0.0, -size, size).astype(jnp.float16)
+
+
+def unpressed(value, power, scale):
+    root = value.astype(jnp.float32) * (1.0 / scale)
+    return root * jnp.abs(root) if power == 2 else root * root * root
 
 
 def parts(value, count):
@@ -93,7 +107,8 @@
     return jnp.concatenate(parts(jnp.concatenate(pieces, axis=1), 2), axis=0)
 
 
-def build_kernel(rows_ref, cols_ref, tile_ref, product_ref, left, right, probes, held, sems):
+def build_kernel(rows_ref, cols_ref, tile_ref, product_ref, left, right, probes, even, odd, sems):
+    held = [even, odd]
     for block in range(COLS):
         right[:, block * OWN : (block + 1) * OWN] = operand(cols_ref[block], -10.0, False)
     for some in range(0, ROWS, 4):
@@ -103,27 +118,28 @@
         left[at, :] = operand(scaled, 1.0, True).T
         probes[:, at] = stacked([block[FEAT:] for block in blocks])
 
-    def leave(chunk):
-        slot = chunk % 2
-        return pltpu.make_async_copy(held.at[slot], tile_ref.at[chunk], sems.at[slot])
-
-    def step(chunk, carry):
-        @pl.when(chunk >= 2)
-        def _():
-            leave(chunk - 2).wait()
-
-        cols = pl.ds(pl.multiple_of(chunk * WIDE, WIDE), WIDE)
-        dist = jnp.dot(left[...], right[:, cols], preferred_element_type=jnp.float32)
-        kernel = matern(dist).astype(jnp.bfloat16)
-        held[chunk % 2] = kernel
-        total = jnp.dot(probes[...], kernel, preferred_element_type=jnp.float32)
-        put_product(total, chunk, product_ref)
-        leave(chunk).start()
+    def leave(chunk, slot):
+        return pltpu.make_async_copy(held[slot], tile_ref.at[chunk], sems.at[slot])
+
+    def step(pair, carry):
+        for slot in range(2):
+            chunk = 2 * pair + slot
+
+            @pl.when(pair >= 1)
+            def _():
+                leave(chunk - 2, slot).wait()
+
+            cols = pl.ds(pl.multiple_of(chunk * WIDE, WIDE), WIDE)
+            dist = jnp.dot(left[...], right[:, cols], preferred_element_type=jnp.float32)
+            held[slot][...] = matern(dist).astype(jnp.bfloat16)
+            total = jnp.dot(probes[...], held[slot][...], preferred_element_type=jnp.float32)
+            put_product(total, chunk, product_ref)
+            leave(chunk, slot).start()
         return carry
 
-    lax.fori_loop(0, CHUNKS, step, 0)
-    leave(CHUNKS - 2).wait()
-    leave(CHUNKS - 1).wait()
+    lax.fori_loop(0, CHUNKS // 2, step, 0)
+    for slot in range(2):
+        leave(CHUNKS - 2 + slot, slot).wait()
 
 
 def build(rows, cols):
@@ -139,7 +155,8 @@
             pltpu.VMEM((ROWS * OWN, DEPTH), jnp.bfloat16),
             pltpu.VMEM((DEPTH, COLS * OWN), jnp.bfloat16),
             pltpu.VMEM((2 * RHS, ROWS * OWN), jnp.bfloat16),
-            pltpu.VMEM((2, ROWS * OWN, WIDE), jnp.bfloat16),
+            pltpu.VMEM((ROWS * OWN, WIDE), jnp.bfloat16),
+            pltpu.VMEM((ROWS * OWN, WIDE), jnp.bfloat16),
             pltpu.SemaphoreType.DMA((2,)),
         ],
         compiler_params=pltpu.CompilerParams(vmem_limit_bytes=40 * 2**20),
@@ -181,14 +198,20 @@
 
 def on_device(points, length_scales, noise_level, targets):
     scaled = (points / length_scales[:, None]).astype(jnp.float16)
-    sent = jnp.concatenate([scaled, targets.astype(jnp.float16)], axis=0)
-    cols = spread(scaled, IN_PLANE).astype(jnp.float32)
-    rows = from_rows(sent).astype(jnp.float32)
+    sent = jnp.concatenate([scaled, pressed(targets, 2, 2.0**14)], axis=0)
+    column = spread(sent, ALONG_Z)
+    ready, column = lax.optimization_barrier((copies(scaled, IN_PLANE), column))
+    cols = exchange(ready, IN_PLANE).astype(jnp.float32)
+    rows = from_pair(column)
+    rows = jnp.concatenate(
+        [rows[:, :FEAT].astype(jnp.float32), unpressed(rows[:, FEAT:], 2, 2.0**14)], axis=1
+    )
 
     noise = noise_level[0]
     tile, partials = build(rows, cols)
     first = own_sum(partials) + noise * targets
-    second = own_sum(again(from_rows(first), tile)) + noise * first
+    probes = unpressed(from_pair(spread(pressed(first, 3, 2.0**9), ALONG_Z)), 3, 2.0**9)
+    second = own_sum(again(probes, tile)) + noise * first
 
     pairs = [
         targets * targets,
@@ -199,8 +222,8 @@
     ]
     own = jnp.stack([jnp.sum(pair, axis=1) for pair in pairs]).reshape(1, -1)
     own = jnp.pad(own, ((0, 0), (0, OWN - own.shape[1])))
-    near = jnp.sum(spread(own, IN_PLANE), axis=0)
-    sums = jnp.sum(from_rows(near), axis=0)[0, : 5 * RHS].reshape(5, RHS)
+    near = jnp.sum(spread(own, IN_PLANE_PAIR), axis=0)
+    sums = jnp.sum(spread(near, ALONG_Z), axis=0)[0, : 5 * RHS].reshape(5, RHS)
     norm, curve, square, cross, cubic = sums
     alpha = norm / curve
     norm_next = norm - 2.0 * alpha * curve + alpha * alpha * square

time: 150 us -> 144 us (0.960)
  blocking collectives: 68.4 us -> 91.9 us
  starting transfers between devices: 26 us -> 10.3 us
  waiting for transfers between devices: 24.6 us -> 12.9 us
    all_to_all x4 -> x5, blocking collectives: 49.8 us -> 79.3 us  [exchange(): return lax.all_to_all(pieces, BOTH, 0, 0, axis_index_groups=groups)]
    all_to_all x3 -> x2, starting transfers between devices: 26 us -> 10.3 us  [exchange(): return lax.all_to_all(pieces, BOTH, 0, 0, axis_index_groups=groups)]
    all_to_all x3 -> x2, waiting for transfers between devices: 24.6 us -> 12.9 us  [exchange(): return lax.all_to_all(pieces, BOTH, 0, 0, axis_index_groups=groups)]
    all_gather x3 -> x2, blocking collectives: 18.6 us -> 12.6 us  [from_pair(): lax.all_gather(value, 'blk', axis_index_groups=PAIRS, axis=0, tiled=True)]
  transfers between devices with their start and end apart: 3 -> 2, of which waited for: 3 -> 2; matrix products, arithmetic and copies ran while one was open for 0% -> 0% of each run, Pallas kernels for 0% -> 0%
where the time goes in v3:
time: 144 us
  blocking collectives  91.9 us (64%)
  Pallas kernels  22.7 us (16%)
  waiting for transfers between devices  12.9 us (9%)
  starting transfers between devices  10.3 us (7%)
  other arithmetic  3.61 us (3%)
    all_to_all x5, blocking collectives, exchange(): return lax.all_to_all(pieces, BOTH, 0, 0, axis_index_groups=groups)  79.3 us
    pallas_call x1, Pallas kernels, build(): pl.pallas_call(build_kernel, out_shape=(jax.ShapeDtypeStruct((CHUNKS, ROW...  15.7 us
    all_to_all x2, waiting for transfers between devices, exchange(): return lax.all_to_all(pieces, BOTH, 0, 0, axis_index_groups=groups)  12.9 us
    all_gather x2, blocking collectives, from_pair(): lax.all_gather(value, 'blk', axis_index_groups=PAIRS, axis=0, tiled=True)  12.6 us
    all_to_all x2, starting transfers between devices, exchange(): return lax.all_to_all(pieces, BOTH, 0, 0, axis_index_groups=groups)  10.3 us
    pallas_call x1, Pallas kernels, again(): pl.pallas_call(again_kernel, out_shape=jax.ShapeDtypeStruct((COLS, RHS, O...  6.96 us
  transfers between devices with their start and end apart: 2, of which 2 were waited for; matrix products, arithmetic and copies ran while one was open for 0% of the time, Pallas kernels for 0%

profile of v3, /device:TPU:1, one launch (start us, length us, event | category | flops | bytes accessed | tf_op | source)
XLA Modules:
  0.0 143.7 jit_solution(8430838133470098683)
XLA Ops:
  0.6 0.0 copy-start
  0.6 0.8 fusion
  1.4 0.8 divide_convert_fusion
  2.3 28.1 %all_to_all.35 = f16[16,48,128]{2,1,0:T(8,128)(2,1)S(1)} all-to-all(f16[16,48,128]{2,1,0:T(8,128)(2,1)S(1)} %broadcast_in_dim.13), channel_id=1, replica_groups={{0,32,64,96,2,34,66,98,4,36,68,100,6,38,70,102},{1,33,65,97,3,35,67,99,..., dimensions={0} | all-to-all | bytes 393216 | tf_op jit(solution)/shard_map/all_to_all | solution.py:46
  30.4 0.7 broadcast_in_dim.12
  31.0 6.5 %all_gather.6 = f16[32,48,128]{2,1,0:T(8,128)(2,1)S(1)} all-gather(f16[16,48,128]{2,1,0:T(8,128)(2,1)S(1)} %all_to_all.35), channel_id=1, replica_groups={{0,1},{2,3},{4,5},{6,7},{8,9},{10,11},{12,13},{14,15},{16,17},{18,19},{..., dimensions={0}, use_global_device_ids=true | all-gather | bytes 589824 | tf_op jit(solution)/shard_map/all_gather | solution.py:58
  37.6 0.1 slice_convert_fusion
  37.7 6.8 %all-to-all-start.1 = ((f16[16,32,128]{2,1,0:T(8,128)(2,1)}), f16[16,32,128]{2,1,0:T(8,128)(2,1)S(1)}, u32[]{:S(2)}, u32[]{:S(2)}) async-start(f16[16,32,128]{2,1,0:T(8,128)(2,1)} %broadcast_in_dim.12), calls=%async_computation.1 | async-start | bytes 262144 | tf_op jit(solution)/shard_map/all_to_all | solution.py:46
  44.5 0.1 pad_maximum_fusion.rows_ref
  44.5 6.8 %all-to-all-done.1 = f16[16,32,128]{2,1,0:T(8,128)(2,1)S(1)} async-done(((f16[16,32,128]{2,1,0:T(8,128)(2,1)}), f16[16,32,128]{2,1,0:T(8,128)(2,1)S(1)}, u32[]{:S(2)}, u32[]{:S(2)}) %all-to-all-start.1) | async-done | bytes 131104 | tf_op jit(solution)/shard_map/all_to_all | solution.py:46
  51.3 15.7 %build.1 = (bf16[8,4096,256]{2,1,0:T(8,128)(2,1)}, f32[16,16,128]{2,1,0:T(8,128)}) custom-call(f32[32,48,128]{2,1,0:T(8,128)S(1)} %pad_maximum_fusion.rows_ref, f32[16,32,128]{2,1,0:T(8,128)S(1)} %convert_element_type.27.cols_ref), custom_call_target="tpu_custom_call" | custom-call | tf_op jit(solution)/shard_map/build/pallas_call | solution.py:146
  67.1 3.5 %all-to-all-start.2 = ((f32[16,16,128]{2,1,0:T(8,128)}), f32[16,16,128]{2,1,0:T(8,128)S(1)}, u32[]{:S(2)}, u32[]{:S(2)}) async-start(f32[16,16,128]{2,1,0:T(8,128)} %get-tuple-element.8), calls=%async_computation.2 | async-start | bytes 262144 | tf_op jit(solution)/shard_map/all_to_all | solution.py:46
  71.3 6.2 %all-to-all-done.2 = f32[16,16,128]{2,1,0:T(8,128)S(1)} async-done(((f32[16,16,128]{2,1,0:T(8,128)}), f32[16,16,128]{2,1,0:T(8,128)S(1)}, u32[]{:S(2)}, u32[]{:S(2)}) %all-to-all-start.2) | async-done | bytes 131104 | tf_op jit(solution)/shard_map/all_to_all | solution.py:46
  77.4 0.7 fusion.1
  78.2 16.0 %all_to_all.36 = f16[16,16,128]{2,1,0:T(8,128)(2,1)S(1)} all-to-all(f16[16,16,128]{2,1,0:T(8,128)(2,1)S(1)} %broadcast_in_dim.14), channel_id=1, replica_groups={{0,32,64,96,2,34,66,98,4,36,68,100,6,38,70,102},{1,33,65,97,3,35,67,99,..., dimensions={0} | all-to-all | bytes 131072 | tf_op jit(solution)/shard_map/all_to_all | solution.py:46
  94.2 6.1 %all_gather.7 = f16[32,16,128]{2,1,0:T(8,128)(2,1)S(1)} all-gather(f16[16,16,128]{2,1,0:T(8,128)(2,1)S(1)} %all_to_all.36), channel_id=1, replica_groups={{0,1},{2,3},{4,5},{6,7},{8,9},{10,11},{12,13},{14,15},{16,17},{18,19},{..., dimensions={0}, use_global_device_ids=true | all-gather | bytes 196608 | tf_op jit(solution)/shard_map/all_gather | solution.py:58
  100.3 7.0 %again.1 = f32[16,16,128]{2,1,0:T(8,128)S(1)} custom-call(f32[32,16,128]{2,1,0:T(8,128)S(1)} %multiply_multiply_fusion.probes_ref, bf16[8,4096,256]{2,1,0:T(8,128)(2,1)} %get-tuple-element.9.tile_ref), custom_call_target="tpu_custom_call" | custom-call | tf_op jit(solution)/shard_map/again/pallas_call | solution.py:181
  107.2 9.5 %all_to_all.37 = f32[16,16,128]{2,1,0:T(8,128)S(1)} all-to-all(f32[16,16,128]{2,1,0:T(8,128)S(1)} %again.1), channel_id=1, replica_groups={{0,128,256,384,8,136,264,392,16,144,272,400,24,152,280,408},{1,129,257,..., dimensions={0} | all-to-all | bytes 262144 | tf_op jit(solution)/shard_map/all_to_all | solution.py:46
  116.8 0.0 copy-done
  116.8 0.2 multiply_reduce_fusion
  117.0 0.1 reshape.104
  117.1 11.8 %all_to_all.38 = f32[32,1,128]{2,1,0:T(1,128)S(1)} all-to-all(f32[32,1,128]{2,1,0:T(1,128)S(1)} %broadcast_in_dim.16), channel_id=1, replica_groups={{0,1,128,129,256,257,384,385,8,9,136,137,264,265,392,393,16,17,144,145,..., dimensions={0} | all-to-all | bytes 32768 | tf_op jit(solution)/shard_map/all_to_all | solution.py:46
  129.0 13.8 %all_to_all.39 = f32[16,1,128]{2,1,0:T(1,128)S(1)} all-to-all(f32[16,1,128]{2,1,0:T(1,128)S(1)} %broadcast_in_dim.17), channel_id=1, replica_groups={{0,32,64,96,2,34,66,98,4,36,68,100,6,38,70,102},{1,33,65,97,3,35,67,99,..., dimensions={0} | all-to-all | bytes 16384 | tf_op jit(solution)/shard_map/all_to_all | solution.py:46
  142.8 0.1 fusion.6
  142.9 0.1 fusion.3
  143.0 0.7 multiply_subtract_fusion
  (14 shorter events, 0.3 us)
Async XLA Ops:
  0.6 116.2 %copy-start = (f32[16,128]{1,0:T(8,128)S(1)}, f32[16,128]{1,0:T(8,128)}, u32[]{:S(2)}) copy-start(f32[16,128]{1,0:T(8,128)} %param.7) | copy-start | bytes 24580
  37.7 13.6 %all-to-all-start.1 = ((f16[16,32,128]{2,1,0:T(8,128)(2,1)}), f16[16,32,128]{2,1,0:T(8,128)(2,1)S(1)}, u32[]{:S(2)}, u32[]{:S(2)}) async-start(f16[16,32,128]{2,1,0:T(8,128)(2,1)} %broadcast_in_dim.12), calls=%async_computation.1 | async-start | bytes 262144 | tf_op jit(solution)/shard_map/all_to_all | solution.py:46
  67.1 10.3 %all-to-all-start.2 = ((f32[16,16,128]{2,1,0:T(8,128)}), f32[16,16,128]{2,1,0:T(8,128)S(1)}, u32[]{:S(2)}, u32[]{:S(2)}) async-start(f32[16,16,128]{2,1,0:T(8,128)} %get-tuple-element.8), calls=%async_computation.2 | async-start | bytes 262144 | tf_op jit(solution)/shard_map/all_to_all | solution.py:46

commit v4 on v2

v4 whole, which is shorter than its diff:
```python
import itertools
import math

import jax
import jax.numpy as jnp
from jax import lax
from jax.experimental import pallas as pl
from jax.experimental.pallas import tpu as pltpu
from jax.sharding import PartitionSpec as P

FEAT = 32
RHS = 16
OWN = 128
ROWS = 32
COLS = 16
DEPTH = 144
WIDE = 256
CHUNKS = COLS * OWN // WIDE
STEPS = 29.9
SQRT_FIVE = math.sqrt(5.0)
HELD = 4

BOTH = ("grp", "blk")
SIZES = {"x": 4, "z_lo": 4, "y": 4, "z_hi": 4, "core": 2}
PAIRS = [[2 * i, 2 * i + 1] for i in range(16)]


def groups_along(axes):
    rest = [axis for axis in SIZES if axis not in axes]
    found = []
    for fixed in itertools.product(*[range(SIZES[axis]) for axis in rest]):
        members = []
        for moving in itertools.product(*[range(SIZES[axis]) for axis in axes]):
            place = dict(zip(rest, fixed)) | dict(zip(axes, moving))
            index = 0
            for axis in SIZES:
                index = index * SIZES[axis] + place[axis]
            members.append(index)
        found.append(members)
    return found


ALONG_Z = groups_along(["z_hi", "z_lo"])
IN_PLANE = groups_along(["y", "x"])
IN_PLANE_PAIR = groups_along(["y", "x", "core"])


def exchange(pieces, groups):
    return lax.all_to_all(pieces, BOTH, 0, 0, axis_index_groups=groups)


def copies(value, groups):
    return jnp.broadcast_to(value[None], (len(groups[0]),) + value.shape)


def spread(value, groups):
    return exchange(copies(value, groups), groups)


def from_pair(value):
    return lax.all_gather(value, "blk", axis_index_groups=PAIRS, axis=0, tiled=True)


def even_code(points):
    size = jnp.abs(points) * (STEPS / 6.0)
    whole = jnp.floor(size)
    code = jnp.exp2(whole - 14.0) * (1.0 + (size - whole))
    return jnp.where(points < 0.0, -code, code).astype(jnp.float16)


def even_points(code):
    code = code.astype(jnp.float32)
    whole = jnp.floor(jnp.log2(jnp.abs(code)))
    size = (whole + 13.0 + jnp.abs(code) * jnp.exp2(-whole)) * (6.0 / STEPS)
    return jnp.where(code < 0.0, -size, size)


def two_codes(values):
    high = (values.astype(jnp.bfloat16).astype(jnp.float32) * 2.0**13).astype(jnp.float16)
    low = (values - high.astype(jnp.float32) * 2.0**-13) * 2.0**21
    return [high, low.astype(jnp.float16)]


def from_two_codes(high, low):
    return high.astype(jnp.float32) * 2.0**-13 + low.astype(jnp.float32) * 2.0**-21


def parts(value, count):
    found = []
    for _ in range(count):
        part = value.astype(jnp.bfloat16)
        found.append(part)
        value = value - part.astype(jnp.float32)
    return found


def operand(coords, left):
    high, low = parts(coords, 2)
    kept = high.astype(jnp.float32) + low.astype(jnp.float32)
    pieces = parts(jnp.sum(kept * kept, axis=0, keepdims=True), 3)
    ones = [jnp.ones_like(pieces[0])] * 3
    rest = jnp.zeros((DEPTH - 4 * FEAT - 6, coords.shape[1]), jnp.bfloat16)
    if left:
        rows = [high, low, high, low] + pieces + ones
    else:
        high, low = high * -2.0, low * -2.0
        rows = [high, high, low, low] + ones + pieces
    return jnp.concatenate(rows + [rest], axis=0)


def matern(five_dist2):
    five_dist2 = jnp.maximum(five_dist2, 1e-30)
    spread_ = five_dist2 * lax.rsqrt(five_dist2)
    decay = jnp.exp2(spread_ * (-math.log2(math.e)))
    return ((spread_ + 1.0) + five_dist2 * (1.0 / 3.0)) * decay


def ready_kernel(
    points_ref, scales_ref, noise_ref, targets_ref,
    points_out_ref, targets_out_ref, scales_out_ref, noise_out_ref,
):
    points_out_ref[...] = points_ref[...]
    targets_out_ref[...] = targets_ref[...]
    scales_out_ref[...] = jnp.broadcast_to(scales_ref[...].reshape(1, FEAT), (OWN, FEAT)).T
    noise_out_ref[...] = jnp.full((RHS, OWN), noise_ref[0], jnp.float32)


def make_ready(points, length_scales, noise_level, targets):
    vmem = pl.BlockSpec(memory_space=pltpu.VMEM)
    return pl.pallas_call(
        ready_kernel,
        out_shape=(
            pltpu.VMEM((FEAT, OWN), jnp.float32),
            pltpu.VMEM((RHS, OWN), jnp.float32),
            pltpu.VMEM((FEAT, OWN), jnp.float32),
            pltpu.VMEM((RHS, OWN), jnp.float32),
        ),
        in_specs=[vmem, vmem, pl.BlockSpec(memory_space=pltpu.SMEM), vmem],
        out_specs=(vmem, vmem, vmem, vmem),
        name="ready",
    )(points, length_scales, noise_level, targets)


def put_product(total, chunk, product_ref):
    for block in range(WIDE // OWN):
        product_ref[chunk * (WIDE // OWN) + block] = total[:, block * OWN : (block + 1) * OWN]


def probes_of(pieces):
    return jnp.concatenate([piece.astype(jnp.bfloat16) for piece in pieces], axis=1)


def build_kernel(rows_ref, cols_ref, tile_ref, product_ref, left, right, probes, sems, *held):
    for block in range(COLS):
        right[:, block * OWN : (block + 1) * OWN] = operand(cols_ref[block], False)
    for some in range(0, ROWS, 4):
        blocks = [rows_ref[some + i] for i in range(4)]
        at = slice(some * OWN, (some + 4) * OWN)
        scaled = jnp.concatenate([block[:FEAT] for block in blocks], axis=1)
        left[at, :] = operand(scaled, True).T
        probes[:, at] = probes_of([block[FEAT:] for block in blocks])

    def leave(chunk):
        return pltpu.make_async_copy(held[chunk % HELD], tile_ref.at[chunk], sems.at[chunk % HELD])

    def multiply(chunk):
        kernel = held[chunk % HELD][...]
        total = jnp.dot(probes[...], kernel, preferred_element_type=jnp.float32)
        put_product(total, chunk, product_ref)

    for chunk in range(CHUNKS):
        if chunk >= HELD:
            leave(chunk - HELD).wait()
        cols = slice(chunk * WIDE, (chunk + 1) * WIDE)
        dist = jnp.dot(left[...], right[:, cols], preferred_element_type=jnp.float32)
        held[chunk % HELD][...] = matern(dist).astype(jnp.bfloat16)
        if chunk >= 1:
            multiply(chunk - 1)
        leave(chunk).start()
    multiply(CHUNKS - 1)
    for chunk in range(CHUNKS - HELD, CHUNKS):
        leave(chunk).wait()


def build(rows, cols):
    return pl.pallas_call(
        build_kernel,
        out_shape=(
            jax.ShapeDtypeStruct((CHUNKS, ROWS * OWN, WIDE), jnp.bfloat16),
            jax.ShapeDtypeStruct((COLS, RHS, OWN), jnp.float32),
        ),
        in_specs=[pl.BlockSpec(memory_space=pltpu.VMEM)] * 2,
        out_specs=(pl.BlockSpec(memory_space=pl.ANY), pl.BlockSpec(memory_space=pltpu.VMEM)),
        scratch_shapes=[
            pltpu.VMEM((ROWS * OWN, DEPTH), jnp.bfloat16),
            pltpu.VMEM((DEPTH, COLS * OWN), jnp.bfloat16),
            pltpu.VMEM((RHS, ROWS * OWN), jnp.bfloat16),
            pltpu.SemaphoreType.DMA((HELD,)),
            *[pltpu.VMEM((ROWS * OWN, WIDE), jnp.bfloat16) for _ in range(HELD)],
        ],
        compiler_params=pltpu.CompilerParams(vmem_limit_bytes=40 * 2**20),
        name="build",
    )(rows, cols)


def again_kernel(probes_ref, tile_ref, product_ref, held, sems):
    def fetch(chunk):
        return pltpu.make_async_copy(tile_ref.at[chunk], held.at[chunk], sems.at[chunk])

    for chunk in range(CHUNKS):
        fetch(chunk).start()
    probes = probes_of([probes_ref[i] for i in range(ROWS)])
    for chunk in range(CHUNKS):
        fetch(chunk).wait()
        total = jnp.dot(probes, held[chunk], preferred_element_type=jnp.float32)
        put_product(total, chunk, product_ref)


def again(probes, tile):
    return pl.pallas_call(
        again_kernel,
        out_shape=jax.ShapeDtypeStruct((COLS, RHS, OWN), jnp.float32),
        in_specs=[pl.BlockSpec(memory_space=pltpu.VMEM), pl.BlockSpec(memory_space=pl.ANY)],
        out_specs=pl.BlockSpec(memory_space=pltpu.VMEM),
        scratch_shapes=[
            pltpu.VMEM((CHUNKS, ROWS * OWN, WIDE), jnp.bfloat16),
            pltpu.SemaphoreType.DMA((CHUNKS,)),
        ],
        compiler_params=pltpu.CompilerParams(vmem_limit_bytes=40 * 2**20),
        name="again",
    )(probes, tile)


def own_sum(partials):
    return jnp.sum(exchange(partials, IN_PLANE), axis=0)


def as_row(sums):
    flat = jnp.stack(sums).reshape(1, -1)
    return jnp.pad(flat, ((0, 0), (0, OWN - flat.shape[1])))


def on_device(points, length_scales, noise_level, targets):
    points, targets, scales, noise = make_ready(points, length_scales, noise_level, targets)
    code = even_code(points)
    column = from_pair(spread(jnp.concatenate([code] + two_codes(targets), axis=0), ALONG_Z))
    row_coords = even_points(column[:, :FEAT]) / scales * SQRT_FIVE
    row_targets = from_two_codes(column[:, FEAT : FEAT + RHS], column[:, FEAT + RHS :])
    rows = jnp.concatenate([row_coords, row_targets], axis=1)
    code, rows = lax.optimization_barrier((code, rows))
    cols = even_points(spread(code, IN_PLANE)) / scales * SQRT_FIVE
    row_targets = rows[:, FEAT:]

    tile, partials = build(rows, cols)
    image = own_sum(partials) + noise * targets
    row_image = from_pair(spread(image, ALONG_Z))

    norm = jnp.sum(row_targets * row_targets, axis=(0, 2))
    curve = jnp.sum(row_targets * row_image, axis=(0, 2))
    square = jnp.sum(row_image * row_image, axis=(0, 2))
    sums = jnp.sum(spread(as_row([norm, curve, square]), IN_PLANE), axis=0)
    norm, curve, square = sums[0, : 3 * RHS].reshape(3, RHS)
    alpha = norm / curve
    norm_next = norm - 2.0 * alpha * curve + alpha * alpha * square
    ratio = (norm_next / norm)[:, None]
    alpha = alpha[:, None]

    row_direction = (row_targets - alpha * row_image) + ratio * row_targets
    partials = again(row_direction, tile)
    residual = targets - alpha * image
    direction = residual + ratio * targets
    image_next = own_sum(partials) + noise * direction
    near = jnp.sum(spread(as_row([jnp.sum(direction * image_next, axis=1)]), IN_PLANE_PAIR), axis=0)
    curve_next = jnp.sum(spread(near, ALONG_Z), axis=0)[0, :RHS]
    alpha_next = (norm_next / curve_next)[:, None]
    solution_field = alpha * targets + alpha_next * direction
    residual = residual - alpha_next * image_next
    return (solution_field, residual)


def solution(mesh):
    return jax.shard_map(
        on_device,
        mesh=mesh,
        in_specs=(P(None, BOTH), P(), P(), P(None, BOTH)),
        out_specs=(P(None, BOTH), P(None, BOTH)),
        check_vma=False,
    )
```

time: 150 us -> 156 us (1.040)
  blocking collectives: 68.4 us -> 130 us
  starting transfers between devices: 26 us -> 0 us
  waiting for transfers between devices: 24.6 us -> 0 us
  Pallas kernels: 23.9 us -> 21.6 us
    all_to_all x4 -> x8, blocking collectives: 49.8 us -> 116 us  [exchange(): return lax.all_to_all(pieces, BOTH, 0, 0, axis_index_groups=groups)]
    all_to_all x3 -> x0, starting transfers between devices: 26 us -> none  [exchange(): return lax.all_to_all(pieces, BOTH, 0, 0, axis_index_groups=groups)]
    all_to_all x3 -> x0, waiting for transfers between devices: 24.6 us -> none  [exchange(): return lax.all_to_all(pieces, BOTH, 0, 0, axis_index_groups=groups)]
    all_gather x3 -> x2, blocking collectives: 18.6 us -> 14.1 us  [from_pair(): lax.all_gather(value, 'blk', axis_index_groups=PAIRS, axis=0, tiled=True)]
    pallas_call x1, Pallas kernels: 16.9 us -> 13.9 us  [build(): pl.pallas_call(build_kernel, out_shape=(jax.ShapeDtypeStruct((CHUNKS, ROW...]
  transfers between devices with their start and end apart: 3 -> 0, of which waited for: 3 -> 0; matrix products, arithmetic and copies ran while one was open for 0% -> 0% of each run, Pallas kernels for 0% -> 0%
where the time goes in v4:
time: 156 us; the launch traced here: 155 us
  blocking collectives  130 us (83%)
  Pallas kernels  21.6 us (14%)
  other arithmetic  2.01 us (1%)
    all_to_all x8, blocking collectives, exchange(): return lax.all_to_all(pieces, BOTH, 0, 0, axis_index_groups=groups)  116 us
    all_gather x2, blocking collectives, from_pair(): lax.all_gather(value, 'blk', axis_index_groups=PAIRS, axis=0, tiled=True)  14.1 us
    pallas_call x1, Pallas kernels, build(): pl.pallas_call(build_kernel, out_shape=(jax.ShapeDtypeStruct((CHUNKS, ROW...  13.9 us
    pallas_call x1, Pallas kernels, again(): pl.pallas_call(again_kernel, out_shape=jax.ShapeDtypeStruct((COLS, RHS, O...  6.91 us

profile of v4, /device:TPU:1, one launch (start us, length us, event | category | flops | bytes accessed | tf_op | source)
XLA Modules:
  0.0 155.4 jit_solution(12792233895759504866)
XLA Ops:
  1.3 0.8 ready.1
  2.2 28.7 %all_to_all.40 = f16[16,64,128]{2,1,0:T(8,128)(2,1)S(1)} all-to-all(f16[16,64,128]{2,1,0:T(8,128)(2,1)S(1)} %broadcast_in_dim.16), channel_id=1, replica_groups={{0,32,64,96,2,34,66,98,4,36,68,100,6,38,70,102},{1,33,65,97,3,35,67,99,..., dimensions={0} | all-to-all | bytes 524288 | tf_op jit(solution)/shard_map/all_to_all | solution.py:49
  30.9 8.0 %all_gather.6 = f16[32,64,128]{2,1,0:T(8,128)(2,1)S(1)} all-gather(f16[16,64,128]{2,1,0:T(8,128)(2,1)S(1)} %all_to_all.40), channel_id=1, replica_groups={{0,1},{2,3},{4,5},{6,7},{8,9},{10,11},{12,13},{14,15},{16,17},{18,19},{..., dimensions={0}, use_global_device_ids=true | all-gather | bytes 786432 | tf_op jit(solution)/shard_map/all_gather | solution.py:61
  38.9 0.3 fusion.11
  39.2 0.1 pad_maximum_fusion.rows_ref
  39.3 13.4 %all_to_all.41 = f16[16,32,128]{2,1,0:T(8,128)(2,1)S(1)} all-to-all(f16[16,32,128]{2,1,0:T(8,128)(2,1)S(1)} %broadcast_in_dim.17), channel_id=1, replica_groups={{0,128,256,384,8,136,264,392,16,144,272,400,24,152,280,408},{1,129,257,..., dimensions={0} | all-to-all | bytes 262144 | tf_op jit(solution)/shard_map/all_to_all | solution.py:49
  52.7 0.2 fusion.23.cols_ref
  52.9 13.9 %build.1 = (bf16[8,4096,256]{2,1,0:T(8,128)(2,1)}, f32[16,16,128]{2,1,0:T(8,128)S(1)}) custom-call(f32[32,48,128]{2,1,0:T(8,128)S(1)} %pad_maximum_fusion.rows_ref, f32[16,32,128]{2,1,0:T(8,128)S(1)} %fusion.23.cols_ref), custom_call_target="tpu_custom_call" | custom-call | tf_op jit(solution)/shard_map/build/pallas_call | solution.py:186
  66.8 9.9 %all_to_all.42 = f32[16,16,128]{2,1,0:T(8,128)S(1)} all-to-all(f32[16,16,128]{2,1,0:T(8,128)S(1)} %get-tuple-element.15), channel_id=1, replica_groups={{0,128,256,384,8,136,264,392,16,144,272,400,24,152,280,408},{1,129,257,..., dimensions={0} | all-to-all | bytes 262144 | tf_op jit(solution)/shard_map/all_to_all | solution.py:49
  76.8 17.3 %all_to_all.43 = f32[16,16,128]{2,1,0:T(8,128)S(1)} all-to-all(f32[16,16,128]{2,1,0:T(8,128)S(1)} %broadcast_in_dim.18), channel_id=1, replica_groups={{0,32,64,96,2,34,66,98,4,36,68,100,6,38,70,102},{1,33,65,97,3,35,67,99,..., dimensions={0} | all-to-all | bytes 262144 | tf_op jit(solution)/shard_map/all_to_all | solution.py:49
  94.1 6.1 %all_gather.7 = f32[32,16,128]{2,1,0:T(8,128)S(1)} all-gather(f32[16,16,128]{2,1,0:T(8,128)S(1)} %all_to_all.43), channel_id=1, replica_groups={{0,1},{2,3},{4,5},{6,7},{8,9},{10,11},{12,13},{14,15},{16,17},{18,19},{..., dimensions={0}, use_global_device_ids=true | all-gather | bytes 393216 | tf_op jit(solution)/shard_map/all_gather | solution.py:61
  100.2 0.2 multiply_reduce_fusion.2
  100.4 0.1 reshape.118
  100.5 9.2 %all_to_all.44 = f32[16,1,128]{2,1,0:T(1,128)S(1)} all-to-all(f32[16,1,128]{2,1,0:T(1,128)S(1)} %broadcast_in_dim.20), channel_id=1, replica_groups={{0,128,256,384,8,136,264,392,16,144,272,400,24,152,280,408},{1,129,257,..., dimensions={0} | all-to-all | bytes 16384 | tf_op jit(solution)/shard_map/all_to_all | solution.py:49
  109.8 0.1 bitcast_divide_fusion.2
  109.8 0.1 multiply_add_fusion.probes_ref
  110.0 6.9 %again.1 = f32[16,16,128]{2,1,0:T(8,128)S(1)} custom-call(f32[32,16,128]{2,1,0:T(8,128)S(1)} %multiply_add_fusion.probes_ref, bf16[8,4096,256]{2,1,0:T(8,128)(2,1)} %get-tuple-element.17.tile_ref), custom_call_target="tpu_custom_call" | custom-call | tf_op jit(solution)/shard_map/again/pallas_call | solution.py:220
  116.9 9.5 %all_to_all.45 = f32[16,16,128]{2,1,0:T(8,128)S(1)} all-to-all(f32[16,16,128]{2,1,0:T(8,128)S(1)} %again.1), channel_id=1, replica_groups={{0,128,256,384,8,136,264,392,16,144,272,400,24,152,280,408},{1,129,257,..., dimensions={0} | all-to-all | bytes 262144 | tf_op jit(solution)/shard_map/all_to_all | solution.py:49
  126.4 0.2 multiply_reduce_fusion.3
  126.7 13.3 %all_to_all.46 = f32[32,1,128]{2,1,0:T(1,128)S(1)} all-to-all(f32[32,1,128]{2,1,0:T(1,128)S(1)} %broadcast_in_dim.22), channel_id=1, replica_groups={{0,1,128,129,256,257,384,385,8,9,136,137,264,265,392,393,16,17,144,145,..., dimensions={0} | all-to-all | bytes 32768 | tf_op jit(solution)/shard_map/all_to_all | solution.py:49
  140.0 14.7 %all_to_all.47 = f32[16,1,128]{2,1,0:T(1,128)S(1)} all-to-all(f32[16,1,128]{2,1,0:T(1,128)S(1)} %broadcast_in_dim.23), channel_id=1, replica_groups={{0,32,64,96,2,34,66,98,4,36,68,100,6,38,70,102},{1,33,65,97,3,35,67,99,..., dimensions={0} | all-to-all | bytes 16384 | tf_op jit(solution)/shard_map/all_to_all | solution.py:49
  154.7 0.7 multiply_subtract_fusion
  (20 shorter events, 0.3 us)

commit v5 on v4

--- a/solution.py
+++ b/solution.py
@@ -42,7 +42,6 @@
 
 ALONG_Z = groups_along(["z_hi", "z_lo"])
 IN_PLANE = groups_along(["y", "x"])
-IN_PLANE_PAIR = groups_along(["y", "x", "core"])
 
 
 def exchange(pieces, groups):
@@ -203,32 +202,40 @@
     )(rows, cols)
 
 
-def again_kernel(probes_ref, tile_ref, product_ref, held, sems):
+def again_kernel(probes_ref, cols_ref, own_ref, tile_ref, product_ref, held, sems):
     def fetch(chunk):
         return pltpu.make_async_copy(tile_ref.at[chunk], held.at[chunk], sems.at[chunk])
 
     for chunk in range(CHUNKS):
         fetch(chunk).start()
     probes = probes_of([probes_ref[i] for i in range(ROWS)])
+    inner = own_ref[...]
     for chunk in range(CHUNKS):
         fetch(chunk).wait()
         total = jnp.dot(probes, held[chunk], preferred_element_type=jnp.float32)
-        put_product(total, chunk, product_ref)
-
-
-def again(probes, tile):
+        for part in range(WIDE // OWN):
+            block = chunk * (WIDE // OWN) + part
+            piece = total[:, part * OWN : (part + 1) * OWN]
+            product_ref[block, :RHS] = piece
+            inner += piece * cols_ref[block]
+    for block in range(COLS):
+        product_ref[block, RHS:] = inner
+
+
+def again(probes, cols, own, tile):
+    vmem = pl.BlockSpec(memory_space=pltpu.VMEM)
     return pl.pallas_call(
         again_kernel,
-        out_shape=jax.ShapeDtypeStruct((COLS, RHS, OWN), jnp.float32),
-        in_specs=[pl.BlockSpec(memory_space=pltpu.VMEM), pl.BlockSpec(memory_space=pl.ANY)],
-        out_specs=pl.BlockSpec(memory_space=pltpu.VMEM),
+        out_shape=jax.ShapeDtypeStruct((COLS, 2 * RHS, OWN), jnp.float32),
+        in_specs=[vmem, vmem, vmem, pl.BlockSpec(memory_space=pl.ANY)],
+        out_specs=vmem,
         scratch_shapes=[
             pltpu.VMEM((CHUNKS, ROWS * OWN, WIDE), jnp.bfloat16),
             pltpu.SemaphoreType.DMA((CHUNKS,)),
         ],
         compiler_params=pltpu.CompilerParams(vmem_limit_bytes=40 * 2**20),
         name="again",
-    )(probes, tile)
+    )(probes, cols, own, tile)
 
 
 def own_sum(partials):
@@ -242,14 +249,16 @@
 
 def on_device(points, length_scales, noise_level, targets):
     points, targets, scales, noise = make_ready(points, length_scales, noise_level, targets)
-    code = even_code(points)
-    column = from_pair(spread(jnp.concatenate([code] + two_codes(targets), axis=0), ALONG_Z))
-    row_coords = even_points(column[:, :FEAT]) / scales * SQRT_FIVE
-    row_targets = from_two_codes(column[:, FEAT : FEAT + RHS], column[:, FEAT + RHS :])
-    rows = jnp.concatenate([row_coords, row_targets], axis=1)
-    code, rows = lax.optimization_barrier((code, rows))
-    cols = even_points(spread(code, IN_PLANE)) / scales * SQRT_FIVE
+    sent = jnp.concatenate([even_code(points)] + two_codes(targets), axis=0)
+
+    def arrived(blocks):
+        coords = even_points(blocks[:, :FEAT]) / scales * SQRT_FIVE
+        return coords, from_two_codes(blocks[:, FEAT : FEAT + RHS], blocks[:, FEAT + RHS :])
+
+    rows = jnp.concatenate(arrived(from_pair(spread(sent, ALONG_Z))), axis=1)
+    sent, rows = lax.optimization_barrier((sent, rows))
     row_targets = rows[:, FEAT:]
+    cols, col_targets = arrived(spread(sent, IN_PLANE))
 
     tile, partials = build(rows, cols)
     image = own_sum(partials) + noise * targets
@@ -258,20 +267,23 @@
     norm = jnp.sum(row_targets * row_targets, axis=(0, 2))
     curve = jnp.sum(row_targets * row_image, axis=(0, 2))
     square = jnp.sum(row_image * row_image, axis=(0, 2))
-    sums = jnp.sum(spread(as_row([norm, curve, square]), IN_PLANE), axis=0)
-    norm, curve, square = sums[0, : 3 * RHS].reshape(3, RHS)
+    sums = jnp.pad(as_row([norm, curve, square]), ((0, 7), (0, 0)))
+    plane = spread(jnp.concatenate([image, sums], axis=0), IN_PLANE)
+    norm, curve, square = jnp.sum(plane[:, RHS], axis=0)[: 3 * RHS].reshape(3, RHS)
     alpha = norm / curve
     norm_next = norm - 2.0 * alpha * curve + alpha * alpha * square
     ratio = (norm_next / norm)[:, None]
     alpha = alpha[:, None]
 
     row_direction = (row_targets - alpha * row_image) + ratio * row_targets
-    partials = again(row_direction, tile)
+    col_direction = (col_targets - alpha * plane[:, :RHS]) + ratio * col_targets
     residual = targets - alpha * image
     direction = residual + ratio * targets
-    image_next = own_sum(partials) + noise * direction
-    near = jnp.sum(spread(as_row([jnp.sum(direction * image_next, axis=1)]), IN_PLANE_PAIR), axis=0)
-    curve_next = jnp.sum(spread(near, ALONG_Z), axis=0)[0, :RHS]
+    noisy = noise * direction
+    both = own_sum(again(row_direction, col_direction, noisy * direction, tile))
+    image_next = both[:RHS] + noisy
+    inner = as_row([jnp.sum(both[RHS:], axis=1)])
+    curve_next = jnp.sum(from_pair(spread(inner, ALONG_Z)), axis=0)[0, :RHS]
     alpha_next = (norm_next / curve_next)[:, None]
     solution_field = alpha * targets + alpha_next * direction
     residual = residual - alpha_next * image_next

time: 156 us -> 151 us (0.968)
  blocking collectives: 130 us -> 125 us
    all_to_all x8 -> x7, blocking collectives: 116 us -> 105 us  [exchange(): return lax.all_to_all(pieces, BOTH, 0, 0, axis_index_groups=groups)]
    all_gather x2 -> x3, blocking collectives: 14.1 us -> 19.8 us  [from_pair(): lax.all_gather(value, 'blk', axis_index_groups=PAIRS, axis=0, tiled=True)]
where the time goes in v5:
time: 151 us
  blocking collectives  125 us (83%)
  Pallas kernels  21.7 us (14%)
  other arithmetic  2.15 us (1%)
    all_to_all x7, blocking collectives, exchange(): return lax.all_to_all(pieces, BOTH, 0, 0, axis_index_groups=groups)  105 us
    all_gather x3, blocking collectives, from_pair(): lax.all_gather(value, 'blk', axis_index_groups=PAIRS, axis=0, tiled=True)  19.8 us
    pallas_call x1, Pallas kernels, build(): pl.pallas_call(build_kernel, out_shape=(jax.ShapeDtypeStruct((CHUNKS, ROW...  13.9 us
    pallas_call x1, Pallas kernels, again(): pl.pallas_call(again_kernel, out_shape=jax.ShapeDtypeStruct((COLS, 2 * RH...  6.93 us

profile of v5, /device:TPU:1, one launch (start us, length us, event | category | flops | bytes accessed | tf_op | source)
XLA Modules:
  0.0 150.7 jit_solution(4168085742395153675)
XLA Ops:
  1.3 0.8 ready.1
  2.2 28.7 %all_to_all.35 = f16[16,64,128]{2,1,0:T(8,128)(2,1)S(1)} all-to-all(f16[16,64,128]{2,1,0:T(8,128)(2,1)S(1)} %broadcast_in_dim.12), channel_id=1, replica_groups={{0,32,64,96,2,34,66,98,4,36,68,100,6,38,70,102},{1,33,65,97,3,35,67,99,..., dimensions={0} | all-to-all | bytes 524288 | tf_op jit(solution)/shard_map/all_to_all | solution.py:48
  30.9 8.0 %all_gather.9 = f16[32,64,128]{2,1,0:T(8,128)(2,1)S(1)} all-gather(f16[16,64,128]{2,1,0:T(8,128)(2,1)S(1)} %all_to_all.35), channel_id=1, replica_groups={{0,1},{2,3},{4,5},{6,7},{8,9},{10,11},{12,13},{14,15},{16,17},{18,19},{..., dimensions={0}, use_global_device_ids=true | all-gather | bytes 786432 | tf_op jit(solution)/shard_map/all_gather | solution.py:60
  38.9 0.3 fusion.11
  39.2 0.1 pad_maximum_fusion.rows_ref
  39.3 14.7 %all_to_all.36 = f16[16,64,128]{2,1,0:T(8,128)(2,1)S(1)} all-to-all(f16[16,64,128]{2,1,0:T(8,128)(2,1)S(1)} %broadcast_in_dim.13), channel_id=1, replica_groups={{0,128,256,384,8,136,264,392,16,144,272,400,24,152,280,408},{1,129,257,..., dimensions={0} | all-to-all | bytes 524288 | tf_op jit(solution)/shard_map/all_to_all | solution.py:48
  54.0 0.2 fusion.23.cols_ref
  54.2 13.9 %build.1 = (bf16[8,4096,256]{2,1,0:T(8,128)(2,1)}, f32[16,16,128]{2,1,0:T(8,128)S(1)}) custom-call(f32[32,48,128]{2,1,0:T(8,128)S(1)} %pad_maximum_fusion.rows_ref, f32[16,32,128]{2,1,0:T(8,128)S(1)} %fusion.23.cols_ref), custom_call_target="tpu_custom_call" | custom-call | tf_op jit(solution)/shard_map/build/pallas_call | solution.py:185
  68.1 9.4 %all_to_all.37 = f32[16,16,128]{2,1,0:T(8,128)S(1)} all-to-all(f32[16,16,128]{2,1,0:T(8,128)S(1)} %get-tuple-element.15), channel_id=1, replica_groups={{0,128,256,384,8,136,264,392,16,144,272,400,24,152,280,408},{1,129,257,..., dimensions={0} | all-to-all | bytes 262144 | tf_op jit(solution)/shard_map/all_to_all | solution.py:48
  77.6 17.3 %all_to_all.38 = f32[16,16,128]{2,1,0:T(8,128)S(1)} all-to-all(f32[16,16,128]{2,1,0:T(8,128)S(1)} %broadcast_in_dim.14), channel_id=1, replica_groups={{0,32,64,96,2,34,66,98,4,36,68,100,6,38,70,102},{1,33,65,97,3,35,67,99,..., dimensions={0} | all-to-all | bytes 262144 | tf_op jit(solution)/shard_map/all_to_all | solution.py:48
  94.9 6.1 %all_gather.10 = f32[32,16,128]{2,1,0:T(8,128)S(1)} all-gather(f32[16,16,128]{2,1,0:T(8,128)S(1)} %all_to_all.38), channel_id=1, replica_groups={{0,1},{2,3},{4,5},{6,7},{8,9},{10,11},{12,13},{14,15},{16,17},{18,19},{..., dimensions={0}, use_global_device_ids=true | all-gather | bytes 393216 | tf_op jit(solution)/shard_map/all_gather | solution.py:60
  101.0 0.2 multiply_reduce_fusion.2
  101.2 0.1 reshape.28
  101.4 10.0 %all_to_all.39 = f32[16,24,128]{2,1,0:T(8,128)S(1)} all-to-all(f32[16,24,128]{2,1,0:T(8,128)S(1)} %broadcast_in_dim.15), channel_id=1, replica_groups={{0,128,256,384,8,136,264,392,16,144,272,400,24,152,280,408},{1,129,257,..., dimensions={0} | all-to-all | bytes 393216 | tf_op jit(solution)/shard_map/all_to_all | solution.py:48
  111.4 0.1 slice_divide_fusion.1
  111.5 0.1 multiply_add_fusion.probes_ref
  111.6 0.1 fusion.33.own_ref
  111.7 0.1 fusion.25.cols_ref
  111.8 6.9 %again.1 = f32[16,32,128]{2,1,0:T(8,128)S(1)} custom-call(f32[32,16,128]{2,1,0:T(8,128)S(1)} %multiply_add_fusion.probes_ref, f32[16,16,128]{2,1,0:T(8,128)S(1)} %fusion.25.cols_ref, f32[16,128]{1,0:T(8,128)S(1)} %fusion.33.own_ref, bf16[8,4096,256]{2,1,0:T(8,128)(2,1)} %get-tuple-element.17.tile_ref), custom_call_target="tpu_custom_call" | custom-call | tf_op jit(solution)/shard_map/again/pallas_call | solution.py:227
  118.7 10.7 %all_to_all.40 = f32[16,32,128]{2,1,0:T(8,128)S(1)} all-to-all(f32[16,32,128]{2,1,0:T(8,128)S(1)} %again.1), channel_id=1, replica_groups={{0,128,256,384,8,136,264,392,16,144,272,400,24,152,280,408},{1,129,257,..., dimensions={0} | all-to-all | bytes 524288 | tf_op jit(solution)/shard_map/all_to_all | solution.py:48
  129.4 0.1 slice_reduce_fusion
  129.6 14.7 %all_to_all.41 = f32[16,1,128]{2,1,0:T(1,128)S(1)} all-to-all(f32[16,1,128]{2,1,0:T(1,128)S(1)} %broadcast_in_dim.17), channel_id=1, replica_groups={{0,32,64,96,2,34,66,98,4,36,68,100,6,38,70,102},{1,33,65,97,3,35,67,99,..., dimensions={0} | all-to-all | bytes 16384 | tf_op jit(solution)/shard_map/all_to_all | solution.py:48
  144.3 5.7 %all_gather.11 = f32[32,1,128]{2,1,0:T(1,128)S(1)} all-gather(f32[16,1,128]{2,1,0:T(1,128)S(1)} %all_to_all.41), channel_id=1, replica_groups={{0,1},{2,3},{4,5},{6,7},{8,9},{10,11},{12,13},{14,15},{16,17},{18,19},{..., dimensions={0}, use_global_device_ids=true | all-gather | bytes 24576 | tf_op jit(solution)/shard_map/all_gather | solution.py:60
  150.0 0.1 reduce_sum.81
  150.0 0.7 fusion.32
  (17 shorter events, 0.3 us)

commit v6 on v5

--- a/solution.py
+++ b/solution.py
@@ -149,7 +149,7 @@
     return jnp.concatenate([piece.astype(jnp.bfloat16) for piece in pieces], axis=1)
 
 
-def build_kernel(rows_ref, cols_ref, tile_ref, product_ref, left, right, probes, sems, *held):
+def build_kernel(rows_ref, cols_ref, tile_ref, kept_ref, product_ref, left, right, probes, sems, *held):
     for block in range(COLS):
         right[:, block * OWN : (block + 1) * OWN] = operand(cols_ref[block], False)
     for some in range(0, ROWS, 4):
@@ -162,22 +162,26 @@
     def leave(chunk):
         return pltpu.make_async_copy(held[chunk % HELD], tile_ref.at[chunk], sems.at[chunk % HELD])
 
+    def place(chunk):
+        return kept_ref if chunk == CHUNKS - 1 else held[chunk % HELD]
+
     def multiply(chunk):
-        kernel = held[chunk % HELD][...]
+        kernel = place(chunk)[...]
         total = jnp.dot(probes[...], kernel, preferred_element_type=jnp.float32)
         put_product(total, chunk, product_ref)
 
     for chunk in range(CHUNKS):
-        if chunk >= HELD:
+        if HELD <= chunk < CHUNKS - 1:
             leave(chunk - HELD).wait()
         cols = slice(chunk * WIDE, (chunk + 1) * WIDE)
         dist = jnp.dot(left[...], right[:, cols], preferred_element_type=jnp.float32)
-        held[chunk % HELD][...] = matern(dist).astype(jnp.bfloat16)
+        place(chunk)[...] = matern(dist).astype(jnp.bfloat16)
         if chunk >= 1:
             multiply(chunk - 1)
-        leave(chunk).start()
+        if chunk < CHUNKS - 1:
+            leave(chunk).start()
     multiply(CHUNKS - 1)
-    for chunk in range(CHUNKS - HELD, CHUNKS):
+    for chunk in range(CHUNKS - 1 - HELD, CHUNKS - 1):
         leave(chunk).wait()
 
 
@@ -185,11 +189,16 @@
     return pl.pallas_call(
         build_kernel,
         out_shape=(
-            jax.ShapeDtypeStruct((CHUNKS, ROWS * OWN, WIDE), jnp.bfloat16),
+            jax.ShapeDtypeStruct((CHUNKS - 1, ROWS * OWN, WIDE), jnp.bfloat16),
+            pltpu.VMEM((ROWS * OWN, WIDE), jnp.bfloat16),
             jax.ShapeDtypeStruct((COLS, RHS, OWN), jnp.float32),
         ),
         in_specs=[pl.BlockSpec(memory_space=pltpu.VMEM)] * 2,
-        out_specs=(pl.BlockSpec(memory_space=pl.ANY), pl.BlockSpec(memory_space=pltpu.VMEM)),
+        out_specs=(
+            pl.BlockSpec(memory_space=pl.ANY),
+            pl.BlockSpec(memory_space=pltpu.VMEM),
+            pl.BlockSpec(memory_space=pltpu.VMEM),
+        ),
         scratch_shapes=[
             pltpu.VMEM((ROWS * OWN, DEPTH), jnp.bfloat16),
             pltpu.VMEM((DEPTH, COLS * OWN), jnp.bfloat16),
@@ -202,17 +211,19 @@
     )(rows, cols)
 
 
-def again_kernel(probes_ref, cols_ref, own_ref, tile_ref, product_ref, held, sems):
+def again_kernel(probes_ref, cols_ref, own_ref, tile_ref, kept_ref, product_ref, held, sems):
     def fetch(chunk):
         return pltpu.make_async_copy(tile_ref.at[chunk], held.at[chunk], sems.at[chunk])
 
-    for chunk in range(CHUNKS):
+    for chunk in range(CHUNKS - 1):
         fetch(chunk).start()
     probes = probes_of([probes_ref[i] for i in range(ROWS)])
     inner = own_ref[...]
-    for chunk in range(CHUNKS):
-        fetch(chunk).wait()
-        total = jnp.dot(probes, held[chunk], preferred_element_type=jnp.float32)
+    for chunk in [CHUNKS - 1, *range(CHUNKS - 1)]:
+        if chunk < CHUNKS - 1:
+            fetch(chunk).wait()
+        kernel = kept_ref[...] if chunk == CHUNKS - 1 else held[chunk]
+        total = jnp.dot(probes, kernel, preferred_element_type=jnp.float32)
         for part in range(WIDE // OWN):
             block = chunk * (WIDE // OWN) + part
             piece = total[:, part * OWN : (part + 1) * OWN]
@@ -222,20 +233,20 @@
         product_ref[block, RHS:] = inner
 
 
-def again(probes, cols, own, tile):
+def again(probes, cols, own, tile, kept):
     vmem = pl.BlockSpec(memory_space=pltpu.VMEM)
     return pl.pallas_call(
         again_kernel,
         out_shape=jax.ShapeDtypeStruct((COLS, 2 * RHS, OWN), jnp.float32),
-        in_specs=[vmem, vmem, vmem, pl.BlockSpec(memory_space=pl.ANY)],
+        in_specs=[vmem, vmem, vmem, pl.BlockSpec(memory_space=pl.ANY), vmem],
         out_specs=vmem,
         scratch_shapes=[
-            pltpu.VMEM((CHUNKS, ROWS * OWN, WIDE), jnp.bfloat16),
-            pltpu.SemaphoreType.DMA((CHUNKS,)),
+            pltpu.VMEM((CHUNKS - 1, ROWS * OWN, WIDE), jnp.bfloat16),
+            pltpu.SemaphoreType.DMA((CHUNKS - 1,)),
         ],
         compiler_params=pltpu.CompilerParams(vmem_limit_bytes=40 * 2**20),
         name="again",
-    )(probes, cols, own, tile)
+    )(probes, cols, own, tile, pltpu.with_memory_space_constraint(kept, pltpu.VMEM))
 
 
 def own_sum(partials):
@@ -260,7 +271,7 @@
     row_targets = rows[:, FEAT:]
     cols, col_targets = arrived(spread(sent, IN_PLANE))
 
-    tile, partials = build(rows, cols)
+    tile, kept, partials = build(rows, cols)
     image = own_sum(partials) + noise * targets
     row_image = from_pair(spread(image, ALONG_Z))
 
@@ -280,7 +291,7 @@
     residual = targets - alpha * image
     direction = residual + ratio * targets
     noisy = noise * direction
-    both = own_sum(again(row_direction, col_direction, noisy * direction, tile))
+    both = own_sum(again(row_direction, col_direction, noisy * direction, tile, kept))
     image_next = both[:RHS] + noisy
     inner = as_row([jnp.sum(both[RHS:], axis=1)])
     curve_next = jnp.sum(from_pair(spread(inner, ALONG_Z)), axis=0)[0, :RHS]

time: 151 us -> 149 us (0.987)
  Pallas kernels: 21.7 us -> 19.7 us
where the time goes in v6:
time: 149 us
  blocking collectives  125 us (84%)
  Pallas kernels  19.7 us (13%)
  other arithmetic  2.15 us (1%)
    all_to_all x7, blocking collectives, exchange(): return lax.all_to_all(pieces, BOTH, 0, 0, axis_index_groups=groups)  105 us
    all_gather x3, blocking collectives, from_pair(): lax.all_gather(value, 'blk', axis_index_groups=PAIRS, axis=0, tiled=True)  19.8 us
    pallas_call x1, Pallas kernels, build(): pl.pallas_call(build_kernel, out_shape=(jax.ShapeDtypeStruct((CHUNKS - 1,...  12.7 us
    pallas_call x1, Pallas kernels, again(): pl.pallas_call(again_kernel, out_shape=jax.ShapeDtypeStruct((COLS, 2 * RH...  6.27 us

profile of v6, /device:TPU:1, one launch (start us, length us, event | category | flops | bytes accessed | tf_op | source)
XLA Modules:
  0.0 148.8 jit_solution(7640142795355799920)
XLA Ops:
  1.3 0.8 ready.1
  2.2 28.7 %all_to_all.35 = f16[16,64,128]{2,1,0:T(8,128)(2,1)S(1)} all-to-all(f16[16,64,128]{2,1,0:T(8,128)(2,1)S(1)} %broadcast_in_dim.12), channel_id=1, replica_groups={{0,32,64,96,2,34,66,98,4,36,68,100,6,38,70,102},{1,33,65,97,3,35,67,99,..., dimensions={0} | all-to-all | bytes 524288 | tf_op jit(solution)/shard_map/all_to_all | solution.py:48
  30.9 8.0 %all_gather.9 = f16[32,64,128]{2,1,0:T(8,128)(2,1)S(1)} all-gather(f16[16,64,128]{2,1,0:T(8,128)(2,1)S(1)} %all_to_all.35), channel_id=1, replica_groups={{0,1},{2,3},{4,5},{6,7},{8,9},{10,11},{12,13},{14,15},{16,17},{18,19},{..., dimensions={0}, use_global_device_ids=true | all-gather | bytes 786432 | tf_op jit(solution)/shard_map/all_gather | solution.py:60
  38.9 0.3 fusion.11
  39.2 0.1 pad_maximum_fusion.rows_ref
  39.3 14.7 %all_to_all.36 = f16[16,64,128]{2,1,0:T(8,128)(2,1)S(1)} all-to-all(f16[16,64,128]{2,1,0:T(8,128)(2,1)S(1)} %broadcast_in_dim.13), channel_id=1, replica_groups={{0,128,256,384,8,136,264,392,16,144,272,400,24,152,280,408},{1,129,257,..., dimensions={0} | all-to-all | bytes 524288 | tf_op jit(solution)/shard_map/all_to_all | solution.py:48
  54.0 0.2 fusion.23.cols_ref
  54.2 12.7 %build.1 = (bf16[7,4096,256]{2,1,0:T(8,128)(2,1)}, bf16[4096,256]{1,0:T(8,128)(2,1)S(1)}, f32[16,16,128]{2,1,0:T(8,128)S(1)}) custom-call(f32[32,48,128]{2,1,0:T(8,128)S(1)} %pad_maximum_fusion.rows_ref, f32[16,32,128]{2,1,0:T(8,128)S(1)} %fusion.23.cols_ref), custom_call_target="tpu_custom_call" | custom-call | tf_op jit(solution)/shard_map/build/pallas_call | solution.py:189
  66.9 9.4 %all_to_all.37 = f32[16,16,128]{2,1,0:T(8,128)S(1)} all-to-all(f32[16,16,128]{2,1,0:T(8,128)S(1)} %get-tuple-element.16), channel_id=1, replica_groups={{0,128,256,384,8,136,264,392,16,144,272,400,24,152,280,408},{1,129,257,..., dimensions={0} | all-to-all | bytes 262144 | tf_op jit(solution)/shard_map/all_to_all | solution.py:48
  76.3 17.3 %all_to_all.38 = f32[16,16,128]{2,1,0:T(8,128)S(1)} all-to-all(f32[16,16,128]{2,1,0:T(8,128)S(1)} %broadcast_in_dim.14), channel_id=1, replica_groups={{0,32,64,96,2,34,66,98,4,36,68,100,6,38,70,102},{1,33,65,97,3,35,67,99,..., dimensions={0} | all-to-all | bytes 262144 | tf_op jit(solution)/shard_map/all_to_all | solution.py:48
  93.6 6.1 %all_gather.10 = f32[32,16,128]{2,1,0:T(8,128)S(1)} all-gather(f32[16,16,128]{2,1,0:T(8,128)S(1)} %all_to_all.38), channel_id=1, replica_groups={{0,1},{2,3},{4,5},{6,7},{8,9},{10,11},{12,13},{14,15},{16,17},{18,19},{..., dimensions={0}, use_global_device_ids=true | all-gather | bytes 393216 | tf_op jit(solution)/shard_map/all_gather | solution.py:60
  99.8 0.2 multiply_reduce_fusion.2
  100.0 0.1 reshape.28
  100.1 10.0 %all_to_all.39 = f32[16,24,128]{2,1,0:T(8,128)S(1)} all-to-all(f32[16,24,128]{2,1,0:T(8,128)S(1)} %broadcast_in_dim.15), channel_id=1, replica_groups={{0,128,256,384,8,136,264,392,16,144,272,400,24,152,280,408},{1,129,257,..., dimensions={0} | all-to-all | bytes 393216 | tf_op jit(solution)/shard_map/all_to_all | solution.py:48
  110.1 0.1 slice_divide_fusion.1
  110.2 0.1 multiply_add_fusion.probes_ref
  110.3 0.1 fusion.33.own_ref
  110.4 0.1 fusion.25.cols_ref
  110.5 6.3 %again.1 = f32[16,32,128]{2,1,0:T(8,128)S(1)} custom-call(f32[32,16,128]{2,1,0:T(8,128)S(1)} %multiply_add_fusion.probes_ref, f32[16,16,128]{2,1,0:T(8,128)S(1)} %fusion.25.cols_ref, f32[16,128]{1,0:T(8,128)S(1)} %fusion.33.own_ref, bf16[7,4096,256]{2,1,0:T(8,128)(2,1)} %get-tuple-element.18.tile_ref, bf16[4096,256]{1,0:T(8,128)(2,1)S(1)} %get-tuple-element.19.kept_ref), custom_call_target="tpu_custom_call" | custom-call | tf_op jit(solution)/shard_map/again/pallas_call | solution.py:238
  116.8 10.7 %all_to_all.40 = f32[16,32,128]{2,1,0:T(8,128)S(1)} all-to-all(f32[16,32,128]{2,1,0:T(8,128)S(1)} %again.1), channel_id=1, replica_groups={{0,128,256,384,8,136,264,392,16,144,272,400,24,152,280,408},{1,129,257,..., dimensions={0} | all-to-all | bytes 524288 | tf_op jit(solution)/shard_map/all_to_all | solution.py:48
  127.5 0.1 slice_reduce_fusion
  127.6 14.7 %all_to_all.41 = f32[16,1,128]{2,1,0:T(1,128)S(1)} all-to-all(f32[16,1,128]{2,1,0:T(1,128)S(1)} %broadcast_in_dim.17), channel_id=1, replica_groups={{0,32,64,96,2,34,66,98,4,36,68,100,6,38,70,102},{1,33,65,97,3,35,67,99,..., dimensions={0} | all-to-all | bytes 16384 | tf_op jit(solution)/shard_map/all_to_all | solution.py:48
  142.3 5.7 %all_gather.11 = f32[32,1,128]{2,1,0:T(1,128)S(1)} all-gather(f32[16,1,128]{2,1,0:T(1,128)S(1)} %all_to_all.41), channel_id=1, replica_groups={{0,1},{2,3},{4,5},{6,7},{8,9},{10,11},{12,13},{14,15},{16,17},{18,19},{..., dimensions={0}, use_global_device_ids=true | all-gather | bytes 24576 | tf_op jit(solution)/shard_map/all_gather | solution.py:60
  148.0 0.1 reduce_sum.81
  148.1 0.7 fusion.32
  (17 shorter events, 0.3 us)
